TPU v7x, 256 devices: a whole 4x4x8 slice. The times are simulated.
256 devices in a mesh: region: 8 (over z), plant: 32 (over x, y, core).
Axes of the slice: x: 4, y: 4, z: 8, core: 2. Of those that a mesh axis runs over, the one named last changes fastest.
Arguments:
- dispatch_start: float32 [16384, 288], P(('region', 'plant')), may hold values from 0 to 1
- marginal_cost: float32 [16384], P(('region', 'plant')), may hold values from 0.3 to 3
- quad_cost: float32 [16384], P(('region', 'plant')), may hold values from 0.5 to 2
- capacity: float32 [16384], P(('region', 'plant')), may hold values from 0.5 to 4
- band_widths: int32 [16384], P(('region', 'plant')), may hold values from 1 to 12
- ramp_band: float32 [25, 288], replicated, may hold values from -0.12 to 0.12
- plant_bus: int32 [16384], P(('region', 'plant')), may hold values from 0 to 2047
- plant_counts: int32 [256], P(('region', 'plant')), may hold values from 8 to 64, as said below
- load: float32 [16384, 288], P('region'), may hold values from -6 to 6
- ptdf: bfloat16 [16384, 16384], P('plant', 'region'), may hold values from -0.046875 to 0.046875
- line_limit: float32 [16384, 288], P('plant'), may hold values from 0.5 to 4
- line_price_start: float32 [16384, 288], P('plant'), may hold values from -3 to 3
- bus_price_start: float32 [16384, 288], P(('region', 'plant')), may hold values from 0 to 2
- energy_price: float32 [288], replicated, may hold values from 0.5 to 3
Outputs:
- dispatch: float32 [16384, 288], P(('region', 'plant'))
- line_price: float32 [16384, 288], P('plant')
- bus_price: float32 [16384, 288], P(('region', 'plant'))
Inputs may be any that keep to these rules, and one draw needn't show every extreme that they name: `plant_counts`: number of live plants in each block of 64 plant slots, live slots first; some block is full in every draw. `plant_bus`: bus of plant i among the 2048 buses of region i // 2048.
All inputs are finite; a program needn't handle non-finite values.
Results may differ from a plain program's by a relative error of at most 0.0037.
Values may be sent and summed in bfloat16 or wider, within the bound.
A program may use at most 64 MiB of HBM per device.

v0:
```python
import jax
import jax.numpy as jnp
from jax import lax
from jax.sharding import PartitionSpec as P

ITERS = 3
OUTER = 2


STEP_SIZE = 0.5


def ramp_band_apply(values, band_table, widths):
    reach = (band_table.shape[0] - 1) // 2
    length = values.shape[1]
    padded = jnp.pad(values, ((0, 0), (reach, reach)))
    result = (1.0 + band_table[reach])[None, :] * values
    for offset in range(1, reach + 1):
        keep = (widths >= offset).astype(jnp.float32)[:, None]
        later = padded[:, reach + offset : reach + offset + length]
        earlier = padded[:, reach - offset : reach - offset + length]
        result = result + keep * (
            band_table[reach + offset][None, :] * later
            + band_table[reach - offset][None, :] * earlier
        )
    return result


def plant_sweeps(
    dispatch, plant_price, marginal_cost, quad_cost, capacity, band_table, widths, live
):
    for sweep in range(ITERS):
        moved = dispatch + STEP_SIZE * (
            plant_price - marginal_cost[:, None] - quad_cost[:, None] * dispatch
        )
        dispatch = live * jnp.clip(
            ramp_band_apply(moved, band_table, widths), 0.0, capacity[:, None]
        )
    return dispatch


def soft_limit(line_price, flow, line_limit):
    shifted = line_price + flow
    return shifted - jnp.clip(shifted, -line_limit, line_limit)


def shards(
    dispatch_start,
    marginal_cost,
    quad_cost,
    capacity,
    band_widths,
    ramp_band,
    plant_bus,
    plant_counts,
    load,
    ptdf,
    line_limit,
    line_price_start,
    bus_price_start,
    energy_price,
):
    slot_count = dispatch_start.shape[0]
    bus_count = load.shape[0]
    live = (lax.broadcasted_iota(jnp.int32, (slot_count, 1), 0) < plant_counts[0]).astype(
        jnp.float32
    )
    region_buses = lax.all_gather(plant_bus, "plant", axis=0, tiled=True)
    dispatch = dispatch_start
    line_price = line_price_start
    bus_price = bus_price_start
    for outer in range(OUTER):
        region_prices = lax.all_gather(bus_price, "plant", axis=0, tiled=True)
        plant_price = jnp.take(region_prices, plant_bus, axis=0)
        dispatch = plant_sweeps(
            dispatch, plant_price, marginal_cost, quad_cost, capacity, ramp_band, band_widths, live
        )
        summed = jax.ops.segment_sum(
            lax.all_gather(dispatch, "plant", axis=0, tiled=True),
            region_buses,
            num_segments=bus_count,
        )
        injection = (summed - load).astype(jnp.bfloat16)
        partial_flow = jnp.dot(ptdf, injection, preferred_element_type=jnp.float32)
        flow_total = lax.psum(partial_flow, "region")
        line_price = soft_limit(line_price, flow_total, line_limit)
        sent_price = line_price.astype(jnp.bfloat16)
        congestion = lax.psum_scatter(
            lax.dot_general(
                ptdf, sent_price, (((0,), (0,)), ((), ())), preferred_element_type=jnp.float32
            ),
            "plant",
            scatter_dimension=0,
            tiled=True,
        )
        bus_price = energy_price[None, :] - congestion
    return (dispatch, line_price, bus_price)


def solution(mesh):
    placed = (
        P(("region", "plant"), None),
        P(("region", "plant")),
        P(("region", "plant")),
        P(("region", "plant")),
        P(("region", "plant")),
        P(),
        P(("region", "plant")),
        P(("region", "plant")),
        P("region", None),
        P("plant", "region"),
        P("plant", None),
        P("plant", None),
        P(("region", "plant"), None),
        P(),
    )
    return jax.shard_map(
        shards,
        mesh=mesh,
        in_specs=placed,
        out_specs=(P(("region", "plant"), None), P("plant", None), P(("region", "plant"), None)),
        check_vma=False,
    )
```

profile of v0, /device:TPU:1, one launch (start us, length us, event | category | flops | bytes accessed | tf_op | source)
XLA Modules:
  0.0 619.1 jit_solution(11178160993886687151)
XLA Ops:
  7.2 0.0 copy-start
  7.2 0.0 all-gather.5.cloned.1.call-start
  7.2 0.7 all-gather.5.cloned.1.call-update
  7.9 0.0 all-gather.7.cloned.1.call-start
  8.6 0.7 compare_select_fusion
  9.3 0.9 slice_reduce_fusion.23
  10.2 1.1 add_reduce_fusion
  11.3 0.7 compare_and_fusion
  12.0 0.7 compare_convert_fusion.11
  12.8 52.1 %all-gather.5.cloned.1.call-done = f32[2048,288]{1,0:T(8,128)} async-done(((f32[64,288]{1,0:T(8,128)}), f32[2048,288]{1,0:T(8,128)}) %all-gather.5.cloned.1.call-update) | async-done | bytes 2359312 | tf_op jit(solution)/shard_map/all_gather | solution.py:73
  64.9 2.6 gather_fusion
  67.5 1.0 multiply_add_fusion.5
  68.5 1.6 multiply_add_fusion.4
  70.1 0.0 copy-start.28
  70.1 0.0 copy-start.27
  70.1 1.6 multiply_add_fusion.3
  71.8 2.2 minimum_multiply_fusion.1
  73.9 0.0 all-gather.7.cloned.1.call-update
  74.0 0.0 all-reduce.10.cloned.1.call-start
  74.0 3.4 copy.23
  77.4 0.0 copy-done.6
  77.6 0.6 dynamic-slice
  78.9 0.3 dynamic-update-slice
  79.2 11.1 %all-reduce.6 = s32[2048]{0:T(1024)S(1)} all-reduce(s32[2048]{0:T(1024)S(1)} %dynamic-update-slice), channel_id=1, replica_groups=mesh['region'=8,'plant'=32] {'plant'}, use_global_device_ids=true, to_apply=%add.6 | all-reduce | flops 2048 | bytes 16384
  90.3 33.3 %all-gather.7.cloned.1.call-done = f32[2048,288]{1,0:T(8,128)} async-done(((f32[64,288]{1,0:T(8,128)}), f32[2048,288]{1,0:T(8,128)}) %all-gather.7.cloned.1.call-update) | async-done | bytes 2359312 | tf_op jit(solution)/shard_map/all_gather | solution.py:79
  123.6 15.0 %scatter_custom_fusion = f32[2048,288]{1,0:T(8,128)} fusion(s32[2048]{0:T(1024)S(1)} %all-reduce.6, f32[2048,288]{1,0:T(8,128)} %all-gather.7.cloned.1.call-done, f32[]{:T(128)} %constant.1.clone.1), kind=kCustom, calls=%fused_computation.12 | custom fusion | flops 589824 | bytes 2359808 | tf_op jit(solution)/shard_map/scatter-add | solution.py:78
  138.6 4.8 fusion.7
  143.5 0.0 all-reduce.10.cloned.1.call-update
  143.5 0.0 reduce-scatter.7.cloned.1.call-start
  143.5 68.3 %all-reduce.10.cloned.1.call-done = f32[512,288]{0,1:T(8,128)} async-done(((f32[512,288]{0,1:T(8,128)}), f32[512,288]{0,1:T(8,128)}) %all-reduce.10.cloned.1.call-update) | async-done | bytes 589840 | tf_op jit(solution)/shard_map/psum | solution.py:85
  211.9 3.3 convolution_bitcast_fusion.1
  215.2 3.5 copy.27
  218.6 0.0 reduce-scatter.7.cloned.1.call-update
  218.6 0.0 all-gather.9.cloned.1.call-start
  218.7 89.5 %reduce-scatter.7.cloned.1.call-done = f32[64,288]{1,0:T(8,128)} async-done(((f32[2048,288]{1,0:T(8,128)}), f32[64,288]{1,0:T(8,128)}) %reduce-scatter.7.cloned.1.call-update) | async-done | bytes 73744
  308.2 1.7 copy.28
  309.8 1.7 broadcast_subtract_fusion.1
  311.5 1.7 copy.24
  313.2 0.0 all-gather.9.cloned.1.call-update
  313.2 0.2 all-gather.11.cloned.1.call-start
  313.4 51.5 %all-gather.9.cloned.1.call-done = f32[2048,288]{1,0:T(8,128)} async-done(((f32[64,288]{1,0:T(8,128)}), f32[2048,288]{1,0:T(8,128)}) %all-gather.9.cloned.1.call-update) | async-done | bytes 2359312 | tf_op jit(solution)/shard_map/all_gather | solution.py:73
  364.9 2.7 gather_fusion.1
  367.6 1.7 multiply_add_fusion.2
  369.3 1.7 multiply_add_fusion.1
  371.0 1.7 multiply_add_fusion
  372.7 2.3 minimum_multiply_fusion
  374.9 0.0 all-gather.11.cloned.1.call-update
  375.0 0.0 all-reduce.12.cloned.1.call-start
  375.0 49.6 %all-gather.11.cloned.1.call-done = f32[2048,288]{1,0:T(8,128)} async-done(((f32[64,288]{1,0:T(8,128)}), f32[2048,288]{1,0:T(8,128)}) %all-gather.11.cloned.1.call-update) | async-done | bytes 2359312 | tf_op jit(solution)/shard_map/all_gather | solution.py:79
  424.6 15.0 %scatter_custom_fusion.1 = f32[2048,288]{1,0:T(8,128)} fusion(s32[2048]{0:T(1024)} %copy-done.25, f32[2048,288]{1,0:T(8,128)} %all-gather.11.cloned.1.call-done, f32[]{:T(128)} %constant.1.clone.1), kind=kCustom, calls=%fused_computation.10 | custom fusion | flops 589824 | bytes 2359808 | tf_op jit(solution)/shard_map/scatter-add | solution.py:78
  439.6 4.7 fusion.6
  444.4 0.0 all-reduce.12.cloned.1.call-update
  444.4 0.0 reduce-scatter.9.cloned.1.call-start
  444.5 68.4 %all-reduce.12.cloned.1.call-done = f32[512,288]{0,1:T(8,128)} async-done(((f32[512,288]{0,1:T(8,128)}), f32[512,288]{0,1:T(8,128)}) %all-reduce.12.cloned.1.call-update) | async-done | bytes 589840 | tf_op jit(solution)/shard_map/psum | solution.py:85
  512.9 1.5 minimum_subtract_fusion
  514.4 0.0 copy-start.3
  514.4 0.8 copy-done.3
  515.2 2.2 convolution_bitcast_fusion
  517.4 3.4 copy.29
  520.8 0.0 reduce-scatter.9.cloned.1.call-update
  520.9 89.5 %reduce-scatter.9.cloned.1.call-done = f32[64,288]{1,0:T(8,128)} async-done(((f32[2048,288]{1,0:T(8,128)}), f32[64,288]{1,0:T(8,128)}) %reduce-scatter.9.cloned.1.call-update) | async-done | bytes 73744
  610.4 1.0 copy.30
  611.4 0.1 broadcast_subtract_fusion
  611.5 0.8 copy.26
  (54 shorter events, 0.1 us)
Async XLA Ops:
  7.2 131.5 %copy-start = (bf16[512,2048]{1,0:T(8,128)(2,1)S(1)}, bf16[512,2048]{1,0:T(8,128)(2,1)}, u32[]{:S(2)}) copy-start(bf16[512,2048]{1,0:T(8,128)(2,1)} %param.25) | copy-start | bytes 6291460
  7.2 57.7 %all-gather.5.cloned.1.call-start = ((), (), s32[]{:S(2)}) async-start(), calls=%async_computation.2 | async-start | bytes 3244032 | tf_op jit(solution)/shard_map/all_gather | solution.py:73
  7.9 115.7 %all-gather.7.cloned.1.call-start = ((), (), s32[]{:S(2)}) async-start(), calls=%async_computation.3 | async-start | bytes 3244032 | tf_op jit(solution)/shard_map/all_gather | solution.py:79
  9.3 59.2 %copy-start.26 = (s32[1024]{0:T(1024)}, s32[1024]{0:T(1024)S(1)}, u32[]{:S(2)}) copy-start(s32[1024]{0:T(1024)S(1)} %pad_clamp_fusion) | copy-start | bytes 12292
  10.2 67.3 %copy-start.4 = (f32[288]{0:T(512)}, f32[288]{0:T(512)S(1)}, u32[]{:S(2)}) copy-start(f32[288]{0:T(512)S(1)} %get-tuple-element.33) | copy-start | bytes 3460
  10.2 67.2 %copy-start.5 = (f32[288]{0:T(512)}, f32[288]{0:T(512)S(1)}, u32[]{:S(2)}) copy-start(f32[288]{0:T(512)S(1)} %get-tuple-element.34) | copy-start | bytes 3460
  10.2 67.2 %copy-start.6 = (f32[288]{0:T(512)}, f32[288]{0:T(512)S(1)}, u32[]{:S(2)}) copy-start(f32[288]{0:T(512)S(1)} %get-tuple-element.35) | copy-start | bytes 3460
  10.2 67.2 %copy-start.7 = (f32[288]{0:T(512)}, f32[288]{0:T(512)S(1)}, u32[]{:S(2)}) copy-start(f32[288]{0:T(512)S(1)} %get-tuple-element.36) | copy-start | bytes 3460
  10.2 67.2 %copy-start.8 = (f32[288]{0:T(512)}, f32[288]{0:T(512)S(1)}, u32[]{:S(2)}) copy-start(f32[288]{0:T(512)S(1)} %get-tuple-element.37) | copy-start | bytes 3460
  12.0 65.5 %copy-start.22 = (pred[64]{0:T(512)(128)(4,1)}, pred[64]{0:T(512)(128)(4,1)S(1)}, u32[]{:S(2)}) copy-start(pred[64]{0:T(512)(128)(4,1)S(1)} %compare_and_fusion) | copy-start | bytes 196
  12.7 64.8 %copy-start.9 = (f32[64]{0:T(128)}, f32[64]{0:T(128)S(1)}, u32[]{:S(2)}) copy-start(f32[64]{0:T(128)S(1)} %get-tuple-element.38) | copy-start | bytes 772
  12.7 64.8 %copy-start.10 = (f32[64]{0:T(128)}, f32[64]{0:T(128)S(1)}, u32[]{:S(2)}) copy-start(f32[64]{0:T(128)S(1)} %get-tuple-element.39) | copy-start | bytes 772
  12.7 64.8 %copy-start.11 = (f32[64]{0:T(128)}, f32[64]{0:T(128)S(1)}, u32[]{:S(2)}) copy-start(f32[64]{0:T(128)S(1)} %get-tuple-element.40) | copy-start | bytes 772
  12.7 64.8 %copy-start.12 = (f32[64]{0:T(128)}, f32[64]{0:T(128)S(1)}, u32[]{:S(2)}) copy-start(f32[64]{0:T(128)S(1)} %get-tuple-element.41) | copy-start | bytes 772
  12.7 64.8 %copy-start.13 = (f32[64]{0:T(128)}, f32[64]{0:T(128)S(1)}, u32[]{:S(2)}) copy-start(f32[64]{0:T(128)S(1)} %get-tuple-element.42) | copy-start | bytes 772
  12.7 64.8 %copy-start.14 = (f32[64]{0:T(128)}, f32[64]{0:T(128)S(1)}, u32[]{:S(2)}) copy-start(f32[64]{0:T(128)S(1)} %get-tuple-element.43) | copy-start | bytes 772
  12.7 64.8 %copy-start.15 = (f32[64]{0:T(128)}, f32[64]{0:T(128)S(1)}, u32[]{:S(2)}) copy-start(f32[64]{0:T(128)S(1)} %get-tuple-element.44) | copy-start | bytes 772
  12.7 64.8 %copy-start.16 = (f32[64]{0:T(128)}, f32[64]{0:T(128)S(1)}, u32[]{:S(2)}) copy-start(f32[64]{0:T(128)S(1)} %get-tuple-element.45) | copy-start | bytes 772
  12.7 64.8 %copy-start.17 = (f32[64]{0:T(128)}, f32[64]{0:T(128)S(1)}, u32[]{:S(2)}) copy-start(f32[64]{0:T(128)S(1)} %get-tuple-element.46) | copy-start | bytes 772
  12.8 64.8 %copy-start.18 = (f32[64]{0:T(128)}, f32[64]{0:T(128)S(1)}, u32[]{:S(2)}) copy-start(f32[64]{0:T(128)S(1)} %get-tuple-element.47) | copy-start | bytes 772
  12.8 64.8 %copy-start.19 = (f32[64]{0:T(128)}, f32[64]{0:T(128)S(1)}, u32[]{:S(2)}) copy-start(f32[64]{0:T(128)S(1)} %get-tuple-element.48) | copy-start | bytes 772
  12.8 64.8 %copy-start.20 = (f32[64]{0:T(128)}, f32[64]{0:T(128)S(1)}, u32[]{:S(2)}) copy-start(f32[64]{0:T(128)S(1)} %get-tuple-element.49) | copy-start | bytes 772
  12.8 64.8 %copy-start.21 = (f32[64]{0:T(128)}, f32[64]{0:T(128)S(1)}, u32[]{:S(2)}) copy-start(f32[64]{0:T(128)S(1)} %get-tuple-element.50) | copy-start | bytes 772
  70.1 7.5 %copy-start.28 = (u32[256]{0:T(256)S(1)}, u32[256]{0:T(256)}, u32[]{:S(2)}) copy-start(u32[256]{0:T(256)} %constant.65) | copy-start | bytes 3076
  70.1 8.7 %copy-start.27 = (s32[64]{0:T(128)S(1)}, s32[64]{0:T(128)}, u32[]{:S(2)}) copy-start(s32[64]{0:T(128)} %param.22) | copy-start | bytes 772
  74.0 137.9 %all-reduce.10.cloned.1.call-start = ((), (), s32[]{:S(2)}) async-start(), calls=%async_computation.4 | async-start | bytes 1179648 | tf_op jit(solution)/shard_map/psum | solution.py:85
  90.3 33.3 %copy-start.25 = (s32[2048]{0:T(1024)}, s32[2048]{0:T(1024)S(1)}, u32[]{:S(2)}) copy-start(s32[2048]{0:T(1024)S(1)} %all-reduce.6) | copy-start | bytes 24580
  138.6 73.2 %copy-start.1 = (f32[512,288]{0,1:T(8,128)S(1)}, f32[512,288]{0,1:T(8,128)}, u32[]{:S(2)}) copy-start(f32[512,288]{0,1:T(8,128)} %param.26) | copy-start | bytes 1769476
  138.6 73.2 %copy-start.2 = (f32[512,288]{0,1:T(8,128)S(1)}, f32[512,288]{0,1:T(8,128)}, u32[]{:S(2)}) copy-start(f32[512,288]{0,1:T(8,128)} %param.27) | copy-start | bytes 1769476
  143.5 164.7 %reduce-scatter.7.cloned.1.call-start = ((), (), s32[]{:S(2)}) async-start(), calls=%async_computation.8 | async-start | bytes 3244032
  215.2 94.7 %copy-start.23 = (f32[288]{0:T(512)S(1)}, f32[288]{0:T(512)}, u32[]{:S(2)}) copy-start(f32[288]{0:T(512)} %param.29) | copy-start | bytes 3460
  218.6 146.3 %all-gather.9.cloned.1.call-start = ((), (), s32[]{:S(2)}) async-start(), calls=%async_computation.5 | async-start | bytes 3244032 | tf_op jit(solution)/shard_map/all_gather | solution.py:73
  313.2 111.4 %all-gather.11.cloned.1.call-start = ((), (), s32[]{:S(2)}) async-start(), calls=%async_computation.6 | async-start | bytes 3244032 | tf_op jit(solution)/shard_map/all_gather | solution.py:79
  375.0 137.9 %all-reduce.12.cloned.1.call-start = ((), (), s32[]{:S(2)}) async-start(), calls=%async_computation.7 | async-start | bytes 1179648 | tf_op jit(solution)/shard_map/psum | solution.py:85
  444.4 166.0 %reduce-scatter.9.cloned.1.call-start = ((), (), s32[]{:S(2)}) async-start(), calls=%async_computation.9 | async-start | bytes 3244032
  514.4 0.8 copy-start.3
  517.4 94.0 %copy-start.24 = (f32[288]{0:T(512)S(1)}, f32[288]{0:T(512)}, u32[]{:S(2)}) copy-start(f32[288]{0:T(512)} %param.29) | copy-start | bytes 3460
Sparse Core Ops, SparseCore 0:
  10.6 54.2 all-gather.4
  74.1 49.5 all-gather.6
  143.6 68.2 all-reduce.9
  218.8 89.3 reduce-scatter.6
  313.3 51.5 all-gather.8
  375.1 49.5 all-gather.10
  444.5 68.2 all-reduce.11
  521.0 89.3 reduce-scatter.8
where the time goes:
time: 620 us; the launch traced here: 619 us
  waiting for transfers between devices  503 us (81%)
  other arithmetic  50.1 us (8%)
  local copies, waits for them, and re-layouts  23.3 us (4%)
  between operations  15.9 us (3%)
  matrix products  15.1 us (2%)
  blocking collectives  11.1 us (2%)
    unnamed x10, waiting for transfers between devices  180 us
    psum x2, waiting for transfers between devices, shards(): flow_total = lax.psum(partial_flow, 'region')  137 us
    all_gather x2, waiting for transfers between devices, shards(): region_prices = lax.all_gather(bus_price, 'plant', axis=0, tiled=True)  104 us
    all_gather x2, waiting for transfers between devices, shards(): lax.all_gather(dispatch, 'plant', axis=0, tiled=True)  82.9 us
    scatter-add x2, other arithmetic, shards(): jax.ops.segment_sum(lax.all_gather(dispatch, 'plant', axis=0, tiled=True)...  30 us
    unnamed x67, local copies, waits for them, and re-layouts  15.5 us
  transfers between devices with their start and end apart: 8, of which 8 were waited for; matrix products, arithmetic and copies ran while one was open for 1% of the time, Pallas kernels for 0%

commit v1 on v0

v1 whole, which is shorter than its diff:
```python
import jax
import jax.numpy as jnp
from jax import lax
from jax.experimental import pallas as pl
from jax.experimental.pallas import tpu as pltpu
from jax.sharding import PartitionSpec as P

H = 288
HALF = 144
EXT = 192
REACH = 12
ITERS = 3
ROWS_A = 80
F32 = jnp.float32
BF16 = jnp.bfloat16
HALVES = ((0, ROWS_A), (ROWS_A, HALF - ROWS_A))
HALVES_EXT = ((0, 96), (96, 96))
NN = (((1,), (0,)), ((), ()))
NT = (((1,), (1,)), ((), ()))


def body(
    dispatch_in, bus_price_in, params_in, ramp_in, energy_in, load_in, ptdf_in, limit_in, lp_in,
    dispatch_out, line_out, bus_out,
    stage, xd, xp, rxd, rxp, pmo, rpm, pm, ids, ramp_t, kt, vb, dsp, px, oh,
    pt, q, ld, lim, lps, slim, slps, f0,
    ga, gb0, gb1, fb, rc0, rc1, sa0, sa1, pb, r1a, r1b, t2a, t2b, r2a, r2b,
    halo_s, halo_p, halo_d, fin_s, fin_r, fd_s, fd_r, lr,
    loc, ex_s, ex_r, id_s, id_r, ag_s, ag_r, zs_s, zs_r, rs_s, rs_r,
):
    z = lax.axis_index("region")
    p = lax.axis_index("plant")
    x = p // 8
    y = (p // 2) % 4
    c = p % 2
    other = 1 - c

    def dev(zz, xx, yy, cc):
        return (zz, (xx * 4 + yy) * 2 + cc)

    sibling = dev(z, x, y, other)

    def xn(d):
        return (x + d) % 4

    def yn(d):
        return (y + d) % 4

    def remote(src, dst, send, recv, device):
        return pltpu.make_async_remote_copy(
            src_ref=src, dst_ref=dst, send_sem=send, recv_sem=recv,
            device_id=device, device_id_type=pl.DeviceIdType.MESH,
        )

    sends = []

    def push(src, dst, send, recv, device):
        copy = remote(src, dst, send, recv, device)
        copy.start()
        sends.append(copy)
        return copy

    def drain():
        for copy in sends:
            copy.wait_send()
        sends.clear()

    def arrived(dst, recv):
        remote(dst, dst, ex_s.at[0], recv, sibling).wait_recv()

    own_row = pl.multiple_of(HALF * c, 16)
    other_row = pl.multiple_of(HALF * other, 16)
    line_lane = pl.multiple_of(128 * (z % 4), 128)
    own_block = pl.ds(pl.multiple_of(512 * c, 512), 512)
    local = [
        pltpu.make_async_copy(ptdf_in, pt.at[own_block], loc.at[0]),
        pltpu.make_async_copy(load_in.at[pl.ds(own_row, HALF)], ld, loc.at[1]),
        pltpu.make_async_copy(
            limit_in.at[pl.ds(own_row, HALF), pl.ds(line_lane, 128)], lim, loc.at[2]),
        pltpu.make_async_copy(
            lp_in.at[pl.ds(own_row, HALF), pl.ds(line_lane, 128)], lps, loc.at[3]),
    ]
    for copy in local:
        copy.start()

    barrier = pltpu.get_barrier_semaphore()
    peers = [sibling]
    peers += [dev(z, xn(d), y, c) for d in (1, 2, 3)]
    peers += [dev(z, x, yn(d), c) for d in (1, 2, 3)]
    peers += [dev((z + d) % 8, x, y, c) for d in range(1, 8)]
    for peer in peers:
        pl.semaphore_signal(barrier, inc=1, device_id=peer, device_id_type=pl.DeviceIdType.MESH)

    own_lanes = pl.ds(pl.multiple_of(64 * c, 64), 64)
    own_ext = pl.ds(pl.multiple_of(96 * c, 96), EXT)
    other_ext = pl.ds(pl.multiple_of(96 * other, 96), EXT)
    stage[...] = jnp.zeros_like(stage)
    stage[own_lanes, 0:H] = bus_price_in[...]
    xp[...] = stage[...].T
    rows = params_in[...]
    gap = jnp.zeros_like(rows)
    pmo[...] = jnp.where(
        c == 0, jnp.concatenate([rows, gap], axis=1), jnp.concatenate([gap, rows], axis=1))
    pl.semaphore_wait(barrier, len(peers))
    push(xp.at[other_ext], rxp, ex_s.at[0], ex_r.at[0], sibling)
    push(pmo, rpm, ex_s.at[1], ex_r.at[1], sibling)
    stage[own_lanes, 0:H] = dispatch_in[...]
    xd[...] = stage[...].T
    push(xd.at[other_ext], rxd, ex_s.at[2], ex_r.at[2], sibling)
    push(ptdf_in, pt.at[own_block], ex_s.at[3], ex_r.at[3], sibling)
    push(limit_in.at[pl.ds(other_row, HALF), pl.ds(line_lane, 128)], slim, ex_s.at[4], ex_r.at[4], sibling)
    push(lp_in.at[pl.ds(other_row, HALF), pl.ds(line_lane, 128)], slps, ex_s.at[5], ex_r.at[5], sibling)

    def gather_start(grid, halves, k):
        for part in (0, 1):
            for h, (row, count) in enumerate(halves):
                block = grid.at[x, y, pl.ds(row, count)]
                for i, d in enumerate((2, 1, 3)):
                    along_x = h == part
                    device = dev(z, xn(d), y, c) if along_x else dev(z, x, yn(d), c)
                    push(block, block, ag_s.at[k, 6 * part + 3 * h + i], ag_r.at[k, h, x, y], device)

    def gather_forward(grid, halves, k):
        n = 12
        for d in (1, 3, 2):
            for h, (row, count) in enumerate(halves):
                sx, sy = (xn(d), y) if h == 0 else (x, yn(d))
                block = grid.at[sx, sy, pl.ds(row, count)]
                arrived(block, ag_r.at[k, h, sx, sy])
                for e in (2, 1, 3):
                    device = dev(z, x, yn(e), c) if h == 0 else dev(z, xn(e), y, c)
                    push(block, block, ag_s.at[k, n], ag_r.at[k, h, sx, sy], device)
                    n += 1

    def gather_finish(grid, halves, k):
        for h, (row, count) in enumerate(halves):
            for d in (1, 3, 2):
                sx, sy = (x, yn(d)) if h == 0 else (xn(d), y)
                arrived(grid.at[sx, sy, pl.ds(row, count)], ag_r.at[k, h, sx, sy])
            for d in (1, 3, 2):
                for e in (1, 3, 2):
                    arrived(grid.at[xn(d), yn(e), pl.ds(row, count)], ag_r.at[k, h, xn(d), yn(e)])

    def wide(ref, rows=None):
        if len(ref.shape) == 4:
            return jnp.concatenate([ref[i, j] for i in range(4) for j in range(4)], axis=1)
        return jnp.concatenate([ref[i] for i in range(8)], axis=1)

    arrived(rxp, ex_r.at[0])
    ga[x, y] = (xp[own_ext] + rxp[...]).astype(BF16)
    gather_start(ga, HALVES_EXT, 0)
    arrived(rpm, ex_r.at[1])
    pm[...] = pmo[...] + rpm[...]
    ids[x, y] = pm[...]
    for i, d in enumerate((2, 1, 3)):
        push(ids.at[x, y], ids.at[x, y], id_s.at[i], id_r.at[i], dev(z, xn(d), y, c))

    stage[...] = jnp.zeros_like(stage)
    stage[0:25, 0:H] = ramp_in[...]
    stage[32:33, 0:H] = energy_in[...]
    ramp_t[...] = stage[...].T
    marginal, quad, cap, width, live = (pm[i:i + 1] for i in range(5))
    for d in range(0, REACH + 1):
        keep = (width > d - 0.5).astype(F32)
        for s in ((0,) if d == 0 else (d, -d)):
            row = REACH + s
            column = ramp_t[own_ext, row:row + 1]
            if d == 0:
                kt[row] = jnp.broadcast_to(1.0 + column, (EXT, 128))
            else:
                kt[row] = column * keep
    energy = ramp_t[pl.ds(own_row, HALF), 32:33]

    gather_forward(ga, HALVES_EXT, 0)
    for i, d in enumerate((2, 1, 3)):
        arrived(ids.at[xn(4 - d), y], id_r.at[i])
    for i, d in enumerate((2, 1, 3)):
        push(ids.at[:, y], ids.at[:, y], id_s.at[3 + i], id_r.at[3 + i], dev(z, x, yn(d), c))
    bus_row = lax.broadcasted_iota(jnp.int32, (2048, 128), 0)
    oh[...] = jnp.where(bus_row == pm[5:6].astype(jnp.int32), 1.0, 0.0).astype(BF16)

    for copy in local:
        copy.wait()
    load_half = ld[...].astype(BF16)
    arrived(pt.at[pl.ds(pl.multiple_of(512 * other, 512), 512)], ex_r.at[3])

    def load_flow(i, _):
        block = pt[pl.ds(pl.multiple_of(256 * i, 256), 256)]
        f0[i] = lax.dot_general(load_half, block, NT, preferred_element_type=F32)
        return 0

    lax.fori_loop(0, 4, load_flow, 0)

    for i, d in enumerate((2, 1, 3)):
        arrived(ids.at[:, yn(4 - d)], id_r.at[3 + i])

    def plant_columns(i, _):
        bus = jnp.concatenate(
            [ids[i // 2, 2 * (i % 2), 5:6], ids[i // 2, 2 * (i % 2) + 1, 5:6]], axis=1)
        iota = lax.broadcasted_iota(jnp.int32, (2048, 256), 0)
        one_hot = jnp.where(iota == bus.astype(jnp.int32), 1.0, 0.0).astype(BF16)
        q[:, pl.ds(pl.multiple_of(256 * i, 256), 256)] = jnp.dot(
            pt[...], one_hot, preferred_element_type=F32).astype(BF16)
        return 0

    lax.fori_loop(0, 4, plant_columns, 0)

    arrived(rxd, ex_r.at[2])
    dsp[...] = xd[own_ext] + rxd[...]
    arrived(slim, ex_r.at[4])
    arrived(slps, ex_r.at[5])
    holds = c == z // 4
    limit = jnp.where(holds, lim[...], slim[...])
    line_price = jnp.where(holds, lps[...], slps[...])
    lim[...] = limit
    lps[...] = line_price

    gather_finish(ga, HALVES_EXT, 0)
    drain()
    px[...] = jnp.dot(wide(ga), oh[...], preferred_element_type=F32)
    vb[...] = jnp.zeros_like(vb)

    core_row = pl.multiple_of(48 * c, 16)
    halo_row = pl.multiple_of(48 + 48 * other, 16)
    halo_at = pl.multiple_of(HALF * other, 16)

    def sweep(_, carry):
        d = dsp[...]
        vb[16:16 + EXT] = d + 0.5 * (px[...] - marginal - quad * d)
        for r in range(0, EXT, 64):
            total = kt[REACH, r:r + 64] * vb[16 + r:16 + r + 64]
            for s in range(1, REACH + 1):
                for o in (s, -s):
                    total = total + kt[REACH + o, r:r + 64] * vb[16 + o + r:16 + o + r + 64]
            dsp[r:r + 64] = live * jnp.clip(total, 0.0, cap)
        return carry

    def limit_lines(k, price, grid, sent, received):
        spread = wide(grid)
        for dq in (2, 1, 3, 0):
            pair = (z // 2 + dq) % 4
            block = q[pl.ds(pl.multiple_of(256 * pair, 256), 256)]
            part = lax.dot_general(spread, block, NT, preferred_element_type=F32) - f0[pair]
            for j in (0, 1):
                fb[k, 2 * pair + j] = part[:, 128 * j:128 * j + 128].astype(BF16)
            for j in (0, 1):
                target = 2 * pair + j
                away = (target - z + 8) % 8

                @pl.when(away != 0)
                def _():
                    remote(fb.at[k, target], received.at[z], zs_s.at[k, 0, target], zs_r.at[k, 0, z],
                           dev(target, x, y, c)).start()

        flow = fb[k, z].astype(F32)
        for d in (1, 7, 2, 6, 3, 5, 4):
            source = (z + d) % 8
            arrived(received.at[source], zs_r.at[k, 0, source])
            flow = flow + received[source].astype(F32)
        shifted = price + flow
        new = shifted - jnp.clip(shifted, -lim[...], lim[...])
        sent[z] = new.astype(BF16)
        for d in (4, 3, 5, 2, 6, 1, 7):
            target = (z + d) % 8
            push(sent.at[z], sent.at[z], zs_s.at[k, 1, target], zs_r.at[k, 1, z], dev(target, x, y, c))
        for d in (1, 7, 2, 6, 3, 5, 4):
            source = (z + d) % 8
            arrived(sent.at[source], zs_r.at[k, 1, source])
        for d in range(1, 8):
            target = (z + d) % 8
            remote(fb.at[k, target], received.at[z], zs_s.at[k, 0, target], zs_r.at[k, 0, z],
                   dev(target, x, y, c)).wait_send()
        drain()
        return new

    def congestion(k, sent, matrix):
        spread = wide(sent)
        for d in (2, 1, 3, 0):
            gx = xn(d)
            for h in (0, 1):
                columns = pl.ds(pl.multiple_of(512 * gx + 256 * h, 256), 256)
                part = jnp.dot(spread, matrix[:, columns], preferred_element_type=F32).astype(BF16)
                pb[k, gx, 2 * h] = part[:, 0:128]
                pb[k, gx, 2 * h + 1] = part[:, 128:256]
            if d:
                push(pb.at[k, gx, :, pl.ds(0, ROWS_A)], r1a.at[k, d - 1], rs_s.at[k, 0, d - 1],
                     rs_r.at[k, 0, d - 1], dev(z, gx, y, c))
        for d in (2, 1, 3):
            push(pb.at[k, :, yn(d), pl.ds(ROWS_A, HALF - ROWS_A)], r1b.at[k, d - 1], rs_s.at[k, 1, d - 1],
                 rs_r.at[k, 1, d - 1], dev(z, x, yn(d), c))
        for d in (1, 3, 2):
            arrived(r1a.at[k, d - 1], rs_r.at[k, 0, d - 1])
        tops = {}
        for e in (2, 1, 3, 0):
            total = pb[k, x, yn(e), 0:ROWS_A].astype(F32)
            for d in (1, 2, 3):
                total = total + r1a[k, d - 1, yn(e)].astype(F32)
            if e:
                t2a[k, e - 1] = total.astype(BF16)
                push(t2a.at[k, e - 1], r2a.at[k, e - 1], rs_s.at[k, 2, e - 1], rs_r.at[k, 2, e - 1],
                     dev(z, x, yn(e), c))
        top = total
        for d in (1, 3, 2):
            arrived(r1b.at[k, d - 1], rs_r.at[k, 1, d - 1])
        for e in (2, 1, 3, 0):
            total = pb[k, xn(e), y, ROWS_A:HALF].astype(F32)
            for d in (1, 2, 3):
                total = total + r1b[k, d - 1, xn(e)].astype(F32)
            if e:
                t2b[k, e - 1] = total.astype(BF16)
                push(t2b.at[k, e - 1], r2b.at[k, e - 1], rs_s.at[k, 3, e - 1], rs_r.at[k, 3, e - 1],
                     dev(z, xn(e), y, c))
        low = total
        for d in (1, 3, 2):
            arrived(r2a.at[k, d - 1], rs_r.at[k, 2, d - 1])
            top = top + r2a[k, d - 1].astype(F32)
        for d in (1, 3, 2):
            arrived(r2b.at[k, d - 1], rs_r.at[k, 3, d - 1])
            low = low + r2b[k, d - 1].astype(F32)
        return jnp.concatenate([top, low], axis=0)

    lax.fori_loop(0, ITERS, sweep, 0)
    gb0[x, y] = dsp[pl.ds(core_row, HALF)].astype(BF16)
    gather_start(gb0, HALVES, 1)
    halo_s[1] = dsp[pl.ds(halo_row, 48)]
    push(halo_s.at[1], halo_d, ex_s.at[6], ex_r.at[6], sibling)
    gather_forward(gb0, HALVES, 1)
    lax.fori_loop(4, 8, plant_columns, 0)
    gather_finish(gb0, HALVES, 1)
    lps[...] = limit_lines(0, lps[...], gb0, sa0, rc0)
    price = energy - congestion(0, sa0, q)
    px[pl.ds(core_row, HALF)] = price
    halo_s[0] = px[pl.ds(halo_row, 48)]
    push(halo_s.at[0], halo_p, ex_s.at[7], ex_r.at[7], sibling)
    arrived(halo_d, ex_r.at[6])
    dsp[pl.ds(halo_at, 48)] = halo_d[...]
    arrived(halo_p, ex_r.at[7])
    px[pl.ds(halo_at, 48)] = halo_p[...]

    lax.fori_loop(0, ITERS, sweep, 0)
    own = dsp[pl.ds(core_row, HALF)]
    gb1[x, y] = own.astype(BF16)
    gather_start(gb1, HALVES, 2)
    fd_s[...] = own
    push(fd_s, fd_r, ex_s.at[8], ex_r.at[8], sibling)
    gather_forward(gb1, HALVES, 2)

    def rows_out(mine, theirs):
        gap = jnp.zeros((96, 128), F32)
        first = jnp.where(c == 0, mine, theirs)
        second = jnp.where(c == 0, theirs, mine)
        return jnp.concatenate([first, second, gap], axis=0).T

    arrived(fd_r, ex_r.at[8])
    stage[...] = rows_out(fd_s[...], fd_r[...])
    dispatch_out[...] = stage[own_lanes, 0:H]
    gather_finish(gb1, HALVES, 2)
    limit_lines(1, lps[...], gb1, sa1, rc1)
    other_lines = pl.ds(pl.multiple_of(4 * other, 4), 4)
    push(sa1.at[other_lines], lr, ex_s.at[9], ex_r.at[9], sibling)
    cong = congestion(1, sa1, pt)
    fin_s[...] = energy - cong
    push(fin_s, fin_r, ex_s.at[10], ex_r.at[10], sibling)
    arrived(lr, ex_r.at[9])
    for i in range(4):
        lanes = slice(128 * i, 128 * i + 128)
        line_out[pl.ds(own_row, HALF), lanes] = sa1[4 * c + i].astype(F32)
        line_out[pl.ds(other_row, HALF), lanes] = lr[i].astype(F32)
    arrived(fin_r, ex_r.at[10])
    stage[...] = rows_out(fin_s[...], fin_r[...])
    bus_out[...] = stage[own_lanes, 0:H]
    drain()


def shards(
    dispatch_start, marginal_cost, quad_cost, capacity, band_widths, ramp_band, plant_bus, plant_counts,
    load, ptdf, line_limit, line_price_start, bus_price_start, energy_price,
):
    live = (jnp.arange(64, dtype=jnp.int32) < plant_counts[0]).astype(F32)
    nothing = jnp.zeros((64,), F32)
    params = jnp.stack([
        marginal_cost, quad_cost, capacity, band_widths.astype(F32), live, plant_bus.astype(F32),
        nothing, nothing,
    ])
    vmem = pl.BlockSpec(memory_space=pltpu.VMEM)
    hbm = pl.BlockSpec(memory_space=pl.ANY)
    sem = pltpu.SemaphoreType.DMA

    def v(shape, kind=F32):
        return pltpu.VMEM(shape, kind)

    low = HALF - ROWS_A
    scratch = [
        v((128, 384)), v((384, 128)), v((384, 128)), v((EXT, 128)), v((EXT, 128)),
        v((8, 128)), v((8, 128)), v((8, 128)), v((4, 4, 8, 128)),
        v((384, 128)), v((25, EXT, 128)), v((EXT + 32, 128)), v((EXT, 128)), v((EXT, 128)),
        v((2048, 128), BF16),
        v((1024, 2048), BF16), v((1024, 2048), BF16), v((HALF, 2048)),
        v((HALF, 128)), v((HALF, 128)), v((HALF, 128)), v((HALF, 128)), v((4, HALF, 256)),
        v((4, 4, EXT, 128), BF16), v((4, 4, HALF, 128), BF16), v((4, 4, HALF, 128), BF16),
        v((2, 8, HALF, 128), BF16), v((8, HALF, 128), BF16), v((8, HALF, 128), BF16),
        v((8, HALF, 128), BF16), v((8, HALF, 128), BF16),
        v((2, 4, 4, HALF, 128), BF16),
        v((2, 3, 4, ROWS_A, 128), BF16), v((2, 3, 4, low, 128), BF16),
        v((2, 3, ROWS_A, 128), BF16), v((2, 3, low, 128), BF16),
        v((2, 3, ROWS_A, 128), BF16), v((2, 3, low, 128), BF16),
        v((2, 48, 128)), v((48, 128)), v((48, 128)),
        v((HALF, 128)), v((HALF, 128)), v((HALF, 128)), v((HALF, 128)),
        v((4, HALF, 128), BF16),
        sem((4,)), sem((11,)), sem((11,)), sem((6,)), sem((6,)), sem((3, 30)), sem((3, 2, 4, 4)),
        sem((2, 2, 8)), sem((2, 2, 8)), sem((2, 4, 3)), sem((2, 4, 3)),
    ]
    dispatch, line_price, bus_price = pl.pallas_call(
        body,
        out_shape=(
            jax.ShapeDtypeStruct((64, H), F32),
            jax.ShapeDtypeStruct((H, 512), F32),
            jax.ShapeDtypeStruct((64, H), F32),
        ),
        in_specs=[vmem] * 5 + [hbm] * 4,
        out_specs=(vmem,) * 3,
        scratch_shapes=scratch,
        compiler_params=pltpu.CompilerParams(
            collective_id=0, has_side_effects=True, vmem_limit_bytes=50 * 2**20),
        name="dispatch_window",
    )(
        dispatch_start, bus_price_start, params, ramp_band, energy_price[None], load.T, ptdf,
        line_limit.T, line_price_start.T,
    )
    return dispatch, line_price.T, bus_price


def solution(mesh):
    placed = (
        P(("region", "plant"), None),
        P(("region", "plant")),
        P(("region", "plant")),
        P(("region", "plant")),
        P(("region", "plant")),
        P(),
        P(("region", "plant")),
        P(("region", "plant")),
        P("region", None),
        P("plant", "region"),
        P("plant", None),
        P("plant", None),
        P(("region", "plant"), None),
        P(),
    )
    return jax.shard_map(
        shards,
        mesh=mesh,
        in_specs=placed,
        out_specs=(P(("region", "plant"), None), P("plant", None), P(("region", "plant"), None)),
        check_vma=False,
    )
```

time: 620 us -> 117 us (0.19)
  waiting for transfers between devices: 503 us -> 0 us
  Pallas kernels: 0 us -> 106 us
  other arithmetic: 50.1 us -> 0.68 us
  local copies, waits for them, and re-layouts: 23.3 us -> 8.2 us
  matrix products: 15.1 us -> 0 us
  between operations: 15.9 us -> 1.3 us
  blocking collectives: 11.1 us -> 0 us
    all_gather x4 -> x0, waiting for transfers between devices: 187 us -> none  [the longest x2 104 us: shards(): region_prices = lax.all_gather(bus_price, 'plant', axis=0, tiled=True)]
    unnamed x10 -> x0, waiting for transfers between devices: 180 us -> none
    psum x2 -> x0, waiting for transfers between devices: 137 us -> none  [shards(): flow_total = lax.psum(partial_flow, 'region')]
    pallas_call x0 -> x1, Pallas kernels: none -> 106 us  [shards(): pl.pallas_call(body, out_shape=(jax.ShapeDtypeStruct((64, H), F32), jax.S...]
    scatter-add x2 -> x0, other arithmetic: 30 us -> none  [shards(): jax.ops.segment_sum(lax.all_gather(dispatch, 'plant', axis=0, tiled=True)...]
    dot_general x4 -> x0, matrix products: 15.1 us -> none  [the longest x2 9.57 us: shards(): partial_flow = jnp.dot(ptdf, injection, preferred_element_type=jnp.float32)]
    unnamed x1 -> x0, blocking collectives: 11.1 us -> none
    add x7 -> x0, other arithmetic: 10.4 us -> none  [the longest x6 9.29 us: plant_sweeps(): dispatch + STEP_SIZE * (plant_price - marginal_cost[:, None] - quad_cost[...]
  transfers between devices with their start and end apart: 8 -> 0, of which waited for: 8 -> 0; matrix products, arithmetic and copies ran while one was open for 1% -> 0% of each run, Pallas kernels for 0% -> 0%
where the time goes in v1:
time: 117 us; the launch traced here: 116 us
  Pallas kernels  106 us (91%)
  local copies, waits for them, and re-layouts  8.2 us (7%)
  between operations  1.3 us (1%)
    pallas_call x1, Pallas kernels, shards(): pl.pallas_call(body, out_shape=(jax.ShapeDtypeStruct((64, H), F32), jax.S...  106 us
    unnamed x13, local copies, waits for them, and re-layouts  6.81 us

profile of v1, /device:TPU:1, one launch (start us, length us, event | category | flops | bytes accessed | tf_op | source)
XLA Modules:
  0.0 116.4 jit_solution(14538347023855161815)
XLA Ops:
  1.3 0.7 convert_bitcast_fusion
  2.0 0.7 stack.28.params_in
  2.7 0.7 broadcast_in_dim.3.energy_in
  3.4 0.0 copy-start
  3.4 1.1 copy-done
  4.4 0.0 copy-start.1
  4.4 1.1 copy-done.1
  5.5 0.0 copy-start.2
  5.5 0.9 copy-done.2
  6.4 0.0 copy-start.3
  6.4 0.9 copy-done.3
  7.3 0.0 copy-start.4
  7.3 0.8 copy-done.4
  8.1 106.2 %dispatch_window.1 = (f32[64,288]{1,0:T(8,128)S(1)}, f32[288,512]{1,0:T(8,128)S(1)}, f32[64,288]{1,0:T(8,128)S(1)}) custom-call(f32[64,288]{1,0:T(8,128)S(1)} %copy-done.2, f32[64,288]{1,0:T(8,128)S(1)} %copy-done.3, f32[8,64]{1,0:T(8,128)S(1)} %stack.28.params_in, f32[25,288]{1,0:T(8,128)S(1)} %copy-done.4, f32[1,288]{1,0:T(1,128)S(1)} %broadcast_in_dim.3.energy_in, ...), custom_call_target="tpu_custom_call" | custom-call | tf_op jit(solution)/shard_map/dispatch_window/pallas_call | solution.py:413
  114.3 0.6 copy.21
  114.9 0.8 copy.22
  115.7 0.6 copy.23
  (2 shorter events, 0.0 us)
Async XLA Ops:
  3.4 1.1 copy-start
  4.4 1.1 copy-start.1
  5.5 0.9 copy-start.2
  6.4 0.9 copy-start.3
  7.3 0.8 copy-start.4

commit v2 on v0

v2 whole, which is shorter than its diff:
```python
import jax
import jax.numpy as jnp
from jax import lax
from jax.experimental import pallas as pl
from jax.experimental.pallas import tpu as pltpu
from jax.sharding import PartitionSpec as P

H = 288
HALF = 144
EXT = 192
PARTS = 3
PART = 48
REACH = 12
ITERS = 3
F32 = jnp.float32
BF16 = jnp.bfloat16
NN = (((1,), (0,)), ((), ()))
NT = (((1,), (1,)), ((), ()))
FAR_FIRST = (2, 1, 3)


def body(
    dispatch_in, bus_price_in, marginal_in, quad_in, cap_in, width_in, bus_in, count_in, ramp_in,
    load_in, ptdf_in, limit_in, lp_in,
    dispatch_out, line_out, bus_out,
    dstage, pstage, prow, irow, crow, ramp_v, stage, xd, xp, rxd, rxp, pmo, rpm, pm, ids, ramp_t, kt, vb, dsp, px, oh,
    pt, q, qt, ld, lim, lps, slim, slps, f0, f0full,
    ga, gb, fb, rc, sa, pb, rp,
    halo_s, halo_p, halo_d, fin_s, fin_r, fd_s, fd_r, lr,
    loc, ex_s, ex_r, id_s, id_r, q_s, q_r, ag_s, ag_r, zr_s, zr_r, zg_s, zg_r, rs_s, rs_r,
):
    z = lax.axis_index("region")
    p = lax.axis_index("plant")
    g = p // 2
    x = g // 4
    y = g % 4
    c = p % 2
    other = 1 - c

    def dev(zz, gg, cc):
        return (zz, gg * 2 + cc)

    sibling = dev(z, g, other)

    def chip(dx, dy):
        return ((x + dx) % 4) * 4 + (y + dy) % 4

    others = [(dx, dy) for dx in (2, 1, 3, 0) for dy in (2, 1, 3, 0) if dx or dy]

    def remote(src, dst, send, recv, device):
        return pltpu.make_async_remote_copy(
            src_ref=src, dst_ref=dst, send_sem=send, recv_sem=recv,
            device_id=device, device_id_type=pl.DeviceIdType.MESH,
        )

    def push(src, dst, send, recv, device):
        remote(src, dst, send, recv, device).start()

    def arrived(dst, recv):
        remote(dst, dst, ex_s.at[0], recv, sibling).wait_recv()

    def sent_off(src, send):
        remote(src, src, send, ex_r.at[0], sibling).wait_send()

    def offset(s, core):
        return pl.multiple_of(core * PART * s + (1 - core) * (HALF - PART - PART * s), 16)

    own_row = pl.multiple_of(HALF * c, 16)
    other_row = pl.multiple_of(HALF * other, 16)
    line_lane = pl.multiple_of(128 * (z % 4), 128)
    own_block = pl.ds(pl.multiple_of(512 * c, 512), 512)
    other_block = pl.ds(pl.multiple_of(512 * other, 512), 512)
    small = [(bus_price_in, pstage), (marginal_in, prow.at[0:1]), (quad_in, prow.at[1:2]), (cap_in, prow.at[2:3]),
             (width_in, irow.at[0:1]), (bus_in, irow.at[1:2]), (count_in, crow), (dispatch_in, dstage),
             (ramp_in, ramp_v)]
    large = [
        (load_in, ld),
        (ptdf_in, pt.at[own_block]),
        (limit_in.at[pl.ds(own_row, HALF), pl.ds(line_lane, 128)], lim),
        (lp_in.at[pl.ds(own_row, HALF), pl.ds(line_lane, 128)], lps),
    ]
    local = [pltpu.make_async_copy(src, dst, loc.at[i]) for i, (src, dst) in enumerate(small + large)]
    for copy in local:
        copy.start()

    barrier = pltpu.get_barrier_semaphore()
    peers = [sibling]
    peers += [dev(z, chip(*d), c) for d in others]
    peers += [dev((z + d) % 8, g, c) for d in range(1, 8)]
    for peer in peers:
        pl.semaphore_signal(barrier, inc=1, device_id=peer, device_id_type=pl.DeviceIdType.MESH)

    own_lanes = pl.ds(pl.multiple_of(64 * c, 64), 64)
    own_ext = pl.ds(pl.multiple_of(96 * c, 96), EXT)
    other_ext = pl.ds(pl.multiple_of(96 * other, 96), EXT)
    for copy in local[:len(small)]:
        copy.wait()
    stage[...] = jnp.zeros_like(stage)
    stage[own_lanes, 0:H] = pstage[...]
    xp[...] = stage[...].T
    slot = lax.broadcasted_iota(jnp.int32, (1, 64), 1)
    live_row = jnp.where(slot < crow[0:1, 0:1], 1.0, 0.0).astype(F32)
    rows = jnp.concatenate(
        [prow[...], irow[...].astype(F32), live_row, jnp.zeros((2, 64), F32)], axis=0)
    gap = jnp.zeros_like(rows)
    pmo[...] = jnp.where(
        c == 0, jnp.concatenate([rows, gap], axis=1), jnp.concatenate([gap, rows], axis=1))
    pl.semaphore_wait(barrier, len(peers))
    push(pmo, rpm, ex_s.at[1], ex_r.at[1], sibling)
    push(xp.at[pl.ds(other_row, HALF)], rxp, ex_s.at[0], ex_r.at[0], sibling)
    push(ptdf_in, pt.at[own_block], ex_s.at[3], ex_r.at[3], sibling)
    stage[own_lanes, 0:H] = dstage[...]
    xd[...] = stage[...].T
    push(xd.at[other_ext], rxd, ex_s.at[2], ex_r.at[2], sibling)
    push(limit_in.at[pl.ds(other_row, HALF), pl.ds(line_lane, 128)], slim, ex_s.at[4], ex_r.at[4], sibling)
    push(lp_in.at[pl.ds(other_row, HALF), pl.ds(line_lane, 128)], slps, ex_s.at[5], ex_r.at[5], sibling)

    def gather(grid, s, k):
        for d in others:
            push(grid.at[s, g], grid.at[s, g], ag_s.at[k, s], ag_r.at[k, s], dev(z, chip(*d), c))

    def gathered(grid, s, k):
        arrived(grid.at[s, pl.ds(0, 15)], ag_r.at[k, s])
        return jnp.concatenate([grid[s, i] for i in range(16)], axis=1)

    arrived(rpm, ex_r.at[1])
    pm[...] = pmo[...] + rpm[...]
    ids[g] = pm[...]
    for d in others:
        push(ids.at[g], ids.at[g], id_s.at[0], id_r.at[0], dev(z, chip(*d), c))
    arrived(rxp, ex_r.at[0])
    for s in range(PARTS):
        row = offset(s, c)
        mine = xp[pl.ds(pl.multiple_of(own_row + row, 16), PART)]
        ga[s, g] = (mine + rxp[pl.ds(row, PART)]).astype(BF16)
        gather(ga, s, 0)

    for copy in local[len(small):]:
        copy.wait()
    load_all = ld[...].astype(BF16)
    for j in range(2):
        block = pt[pl.ds(pl.multiple_of(512 * c + 256 * j, 256), 256)]
        f0full[j] = lax.dot_general(load_all, block, NT, preferred_element_type=F32)
        f0[2 * c + j] = f0full[j, pl.ds(own_row, HALF)]
    own_pairs = pl.ds(2 * c, 2)
    push(f0full.at[:, pl.ds(other_row, HALF)], f0.at[own_pairs], ex_s.at[11], ex_r.at[11], sibling)

    stage[...] = jnp.zeros_like(stage)
    stage[0:26, 0:H] = ramp_v[...]
    ramp_t[...] = stage[...].T
    marginal, quad, cap, width = (pm[i:i + 1] for i in range(4))
    live = pm[5:6]
    for d in range(0, REACH + 1):
        keep = (width > d - 0.5).astype(F32)
        for o in ((0,) if d == 0 else (d, -d)):
            row = REACH + o
            column = ramp_t[own_ext, row:row + 1]
            if d == 0:
                kt[row] = jnp.broadcast_to(1.0 + column, (EXT, 128))
            else:
                kt[row] = column * keep
    bus_row = lax.broadcasted_iota(jnp.int32, (2048, 128), 0)
    oh[...] = jnp.where(bus_row == pm[4:5].astype(jnp.int32), 1.0, 0.0).astype(BF16)

    arrived(pt.at[other_block], ex_r.at[3])
    arrived(ids.at[pl.ds(0, 15)], id_r.at[0])

    def plant_columns(j, _):
        i = 4 * c + j
        bus = jnp.concatenate([ids[2 * i, 4:5], ids[2 * i + 1, 4:5]], axis=1)
        iota = lax.broadcasted_iota(jnp.int32, (2048, 256), 0)
        one_hot = jnp.where(iota == bus.astype(jnp.int32), 1.0, 0.0).astype(BF16)
        q[i] = jnp.dot(pt[...], one_hot, preferred_element_type=F32).astype(BF16)
        push(q.at[i], q.at[i], q_s.at[j], q_r.at[j], sibling)
        return 0

    core_row = pl.multiple_of(48 * c, 16)
    halo_at = pl.multiple_of(HALF * other, 16)

    def ext_part(s):
        return pl.ds(pl.multiple_of(core_row + offset(s, c), 16), PART)

    def price_part(s):
        px[ext_part(s)] = jnp.dot(gathered(ga, s, 0), oh[...], preferred_element_type=F32)

    lax.fori_loop(0, 2, plant_columns, 0)
    price_part(0)
    halo_s[0] = px[ext_part(0)]
    push(halo_s.at[0], halo_p.at[0], ex_s.at[6], ex_r.at[6], sibling)
    arrived(rxd, ex_r.at[2])
    dsp[...] = xd[own_ext] + rxd[...]
    lax.fori_loop(2, 4, plant_columns, 0)
    price_part(1)
    arrived(slim, ex_r.at[4])
    arrived(slps, ex_r.at[5])
    holds = c == z // 4
    lim[...] = jnp.where(holds, lim[...], slim[...])
    lps[...] = jnp.where(holds, lps[...], slps[...])
    arrived(f0.at[pl.ds(2 * other, 2)], ex_r.at[11])
    vb[...] = jnp.zeros_like(vb)
    arrived(halo_p.at[0], ex_r.at[6])
    px[pl.ds(halo_at, PART)] = halo_p[0]
    price_part(2)

    def sweep(_, carry):
        d = dsp[...]
        vb[16:16 + EXT] = d + 0.5 * (px[...] - marginal - quad * d)
        for r in range(0, EXT, 64):
            total = kt[REACH, r:r + 64] * vb[16 + r:16 + r + 64]
            for s in range(1, REACH + 1):
                for o in (s, -s):
                    total = total + kt[REACH + o, r:r + 64] * vb[16 + o + r:16 + o + r + 64]
            dsp[r:r + 64] = live * jnp.clip(total, 0.0, cap)
        return carry

    def start_gather(k):
        for s in range(PARTS):
            gb[k, s, g] = dsp[ext_part(s)].astype(BF16)
            gather(gb.at[k], s, 1 + k)

    def flow(k, s):
        spread = gathered(gb.at[k], s, 1 + k)
        rows = pl.ds(offset(s, c), PART)
        for dq in (2, 1, 3, 0):
            pair = (z // 2 + dq) % 4
            part = jnp.dot(spread, qt[pair], preferred_element_type=F32) - f0[pair, rows]
            for j in (0, 1):
                fb[k, s, 2 * pair + j] = part[:, 128 * j:128 * j + 128].astype(BF16)
            for j in (0, 1):
                target = 2 * pair + j

                @pl.when(target != z)
                def _():
                    push(fb.at[k, s, target], rc.at[k, s, z], zr_s.at[k, s], zr_r.at[k, s], dev(target, g, c))

    def limit_lines(k, s):
        arrived(rc.at[k, s, pl.ds(0, 7)], zr_r.at[k, s])
        total = fb[k, s, z].astype(F32)
        for d in range(1, 8):
            total = total + rc[k, s, (z + d) % 8].astype(F32)
        rows = pl.ds(offset(s, c), PART)
        shifted = lps[rows] + total
        limit = lim[rows]
        new = shifted - jnp.clip(shifted, -limit, limit)
        lps[rows] = new
        sa[k, s, z] = new.astype(BF16)
        for d in (4, 3, 5, 2, 6, 1, 7):
            push(sa.at[k, s, z], sa.at[k, s, z], zg_s.at[k, s], zg_r.at[k, s], dev((z + d) % 8, g, c))

    def congestion(k, s):
        arrived(sa.at[k, s, pl.ds(0, 7)], zg_r.at[k, s])
        spread = jnp.concatenate([sa[k, s, i] for i in range(8)], axis=1)
        for dx in (2, 1, 3, 0):
            row = (x + dx) % 4
            for h in (0, 1):
                i = 2 * row + h
                matrix = q[i] if k == 0 else pt[:, pl.ds(pl.multiple_of(256 * i, 256), 256)]
                part = jnp.dot(spread, matrix, preferred_element_type=F32).astype(BF16)
                pb[k, s, 2 * i] = part[:, 0:128]
                pb[k, s, 2 * i + 1] = part[:, 128:256]
            for dy in (2, 1, 3, 0):
                if dx or dy:
                    to = chip(dx, dy)
                    push(pb.at[k, s, to], rp.at[k, s, g], rs_s.at[k, s], rs_r.at[k, s], dev(z, to, c))


    def prices(k, s):
        arrived(rp.at[k, s, pl.ds(0, 15)], rs_r.at[k, s])
        total = pb[k, s, g].astype(F32)
        for d in range(1, 16):
            total = total + rp[k, s, (g + d) % 16].astype(F32)
        row = pl.multiple_of(own_row + offset(s, c), 16)
        return ramp_t[pl.ds(row, PART), 25:26] - total

    lax.fori_loop(0, ITERS, sweep, 0)
    start_gather(0)
    halo_s[1] = dsp[ext_part(0)]
    push(halo_s.at[1], halo_d, ex_s.at[7], ex_r.at[7], sibling)
    for j in range(4):
        arrived(q.at[4 * other + j], q_r.at[j])

    def transpose_columns(i, _):
        for pair in range(4):
            qt[pair, pl.ds(pl.multiple_of(256 * i, 256), 256)] = q[i, 256 * pair:256 * pair + 256].T
        return 0

    lax.fori_loop(0, 8, transpose_columns, 0)
    for s in range(PARTS):
        flow(0, s)
    for s in range(PARTS):
        limit_lines(0, s)
    for s in range(PARTS):
        congestion(0, s)
    for s in range(PARTS):
        px[ext_part(s)] = prices(0, s)
        if s == 0:
            halo_s[2] = px[ext_part(0)]
            push(halo_s.at[2], halo_p.at[1], ex_s.at[8], ex_r.at[8], sibling)
            arrived(halo_d, ex_r.at[7])
            dsp[pl.ds(halo_at, PART)] = halo_d[...]
    arrived(halo_p.at[1], ex_r.at[8])
    px[pl.ds(halo_at, PART)] = halo_p[1]

    lax.fori_loop(0, ITERS, sweep, 0)
    start_gather(1)
    fd_s[...] = dsp[pl.ds(core_row, HALF)]
    push(fd_s, fd_r, ex_s.at[9], ex_r.at[9], sibling)

    def rows_out(mine, theirs):
        gap = jnp.zeros((96, 128), F32)
        first = jnp.where(c == 0, mine, theirs)
        second = jnp.where(c == 0, theirs, mine)
        return jnp.concatenate([first, second, gap], axis=0).T

    arrived(fd_r, ex_r.at[9])
    stage[...] = rows_out(fd_s[...], fd_r[...])
    dispatch_out[...] = stage[own_lanes, 0:H]
    for s in range(PARTS):
        flow(1, s)
    for s in range(PARTS):
        limit_lines(1, s)
    for s in range(PARTS):
        congestion(1, s)
    push(sa.at[1, :, pl.ds(pl.multiple_of(4 * other, 4), 4)], lr, ex_s.at[10], ex_r.at[10], sibling)
    for s in range(PARTS):
        rows = pl.ds(pl.multiple_of(own_row + offset(s, c), 16), PART)
        for i in range(4):
            line_out[rows, 128 * i:128 * i + 128] = sa[1, s, 4 * c + i].astype(F32)
    for s in range(PARTS):
        rows = pl.ds(offset(s, c), PART)
        fin_s[rows] = prices(1, s)
        push(fin_s.at[rows], fin_r.at[rows], ex_s.at[12 + s], ex_r.at[12 + s], sibling)
    arrived(lr, ex_r.at[10])
    for s in range(PARTS):
        rows = pl.ds(pl.multiple_of(other_row + offset(s, other), 16), PART)
        for i in range(4):
            line_out[rows, 128 * i:128 * i + 128] = lr[s, i].astype(F32)
    for s in range(PARTS):
        arrived(fin_r.at[pl.ds(offset(s, other), PART)], ex_r.at[12 + s])
    stage[...] = rows_out(fin_s[...], fin_r[...])
    bus_out[...] = stage[own_lanes, 0:H]

    for ref, i in ((pmo, 1), (rxp, 0), (ptdf_in, 3), (rxd, 2), (slim, 4), (slps, 5), (f0.at[own_pairs], 11),
                   (halo_s.at[0], 6), (halo_s.at[1], 7), (halo_s.at[2], 8), (fd_s, 9), (lr, 10),
                   (fin_s.at[0:PART], 12), (fin_s.at[0:PART], 13), (fin_s.at[0:PART], 14)):
        sent_off(ref, ex_s.at[i])
    sent_off(ids.at[pl.ds(0, 15)], id_s.at[0])
    for j in range(4):
        sent_off(q.at[j], q_s.at[j])
    for s in range(PARTS):
        for k in range(3):
            sent_off(ga.at[s, pl.ds(0, 15), pl.ds(0, PART)], ag_s.at[k, s])
        for k in range(2):
            sent_off(rc.at[k, s, pl.ds(0, 7)], zr_s.at[k, s])
            sent_off(sa.at[k, s, pl.ds(0, 7)], zg_s.at[k, s])
            sent_off(rp.at[k, s, pl.ds(0, 15)], rs_s.at[k, s])


def shards(
    dispatch_start, marginal_cost, quad_cost, capacity, band_widths, ramp_band, plant_bus, plant_counts,
    load, ptdf, line_limit, line_price_start, bus_price_start, energy_price,
):
    ramp = jnp.concatenate([ramp_band, energy_price[None]], axis=0)
    vmem = pl.BlockSpec(memory_space=pltpu.VMEM)
    hbm = pl.BlockSpec(memory_space=pltpu.HBM)
    sem = pltpu.SemaphoreType.DMA

    def v(shape, kind=F32):
        return pltpu.VMEM(shape, kind)

    scratch = [
        v((64, H)), v((64, H)), v((3, 64)), v((2, 64), jnp.int32), v((1, 1), jnp.int32), v((26, H)),
        v((128, 384)), v((384, 128)), v((384, 128)), v((EXT, 128)), v((HALF, 128)),
        v((8, 128)), v((8, 128)), v((8, 128)), v((16, 8, 128)),
        v((384, 128)), v((25, EXT, 128)), v((EXT + 32, 128)), v((EXT, 128)), v((EXT, 128)),
        v((2048, 128), BF16),
        v((1024, 2048), BF16), v((8, 1024, 256), BF16), v((4, 2048, 256), BF16), v((H, 2048)),
        v((HALF, 128)), v((HALF, 128)), v((HALF, 128)), v((HALF, 128)),
        v((4, HALF, 256)), v((2, H, 256)),
        v((PARTS, 16, PART, 128), BF16), v((2, PARTS, 16, PART, 128), BF16),
        v((2, PARTS, 8, PART, 128), BF16), v((2, PARTS, 8, PART, 128), BF16),
        v((2, PARTS, 8, PART, 128), BF16),
        v((2, PARTS, 16, PART, 128), BF16), v((2, PARTS, 16, PART, 128), BF16),
        v((3, PART, 128)), v((2, PART, 128)), v((PART, 128)),
        v((HALF, 128)), v((HALF, 128)), v((HALF, 128)), v((HALF, 128)),
        v((PARTS, 4, PART, 128), BF16),
        sem((13,)), sem((15,)), sem((15,)), sem((1,)), sem((1,)), sem((4,)), sem((4,)),
        sem((3, PARTS)), sem((3, PARTS)), sem((2, PARTS)), sem((2, PARTS)), sem((2, PARTS)), sem((2, PARTS)),
        sem((2, PARTS)), sem((2, PARTS)),
    ]
    dispatch, line_price, bus_price = pl.pallas_call(
        body,
        out_shape=(
            jax.ShapeDtypeStruct((64, H), F32),
            jax.ShapeDtypeStruct((H, 512), F32),
            jax.ShapeDtypeStruct((64, H), F32),
        ),
        in_specs=[hbm] * 13,
        out_specs=(vmem,) * 3,
        scratch_shapes=scratch,
        compiler_params=pltpu.CompilerParams(
            collective_id=0, has_side_effects=True, vmem_limit_bytes=56 * 2**20),
        name="dispatch_window",
    )(
        dispatch_start, bus_price_start, marginal_cost[None], quad_cost[None], capacity[None],
        band_widths[None], plant_bus[None], plant_counts[None], ramp, load.T, ptdf, line_limit.T,
        line_price_start.T,
    )
    return dispatch, line_price.T, bus_price


def solution(mesh):
    placed = (
        P(("region", "plant"), None),
        P(("region", "plant")),
        P(("region", "plant")),
        P(("region", "plant")),
        P(("region", "plant")),
        P(),
        P(("region", "plant")),
        P(("region", "plant")),
        P("region", None),
        P("plant", "region"),
        P("plant", None),
        P("plant", None),
        P(("region", "plant"), None),
        P(),
    )
    return jax.shard_map(
        shards,
        mesh=mesh,
        in_specs=placed,
        out_specs=(P(("region", "plant"), None), P("plant", None), P(("region", "plant"), None)),
        check_vma=False,
    )
```

time: 620 us -> 89.6 us (0.14)
  waiting for transfers between devices: 503 us -> 0 us
  Pallas kernels: 0 us -> 80.9 us
  other arithmetic: 50.1 us -> 1.43 us
  local copies, waits for them, and re-layouts: 23.3 us -> 5.68 us
  matrix products: 15.1 us -> 0 us
  between operations: 15.9 us -> 1.29 us
  blocking collectives: 11.1 us -> 0 us
    all_gather x4 -> x0, waiting for transfers between devices: 187 us -> none  [the longest x2 104 us: shards(): region_prices = lax.all_gather(bus_price, 'plant', axis=0, tiled=True)]
    unnamed x10 -> x0, waiting for transfers between devices: 180 us -> none
    psum x2 -> x0, waiting for transfers between devices: 137 us -> none  [shards(): flow_total = lax.psum(partial_flow, 'region')]
    pallas_call x0 -> x1, Pallas kernels: none -> 80.9 us  [shards(): pl.pallas_call(body, out_shape=(jax.ShapeDtypeStruct((64, H), F32), jax.S...]
    scatter-add x2 -> x0, other arithmetic: 30 us -> none  [shards(): jax.ops.segment_sum(lax.all_gather(dispatch, 'plant', axis=0, tiled=True)...]
    dot_general x4 -> x0, matrix products: 15.1 us -> none  [the longest x2 9.57 us: shards(): partial_flow = jnp.dot(ptdf, injection, preferred_element_type=jnp.float32)]
    unnamed x1 -> x0, blocking collectives: 11.1 us -> none
    unnamed x67 -> x3, local copies, waits for them, and re-layouts: 15.5 us -> 4.99 us
  transfers between devices with their start and end apart: 8 -> 0, of which waited for: 8 -> 0; matrix products, arithmetic and copies ran while one was open for 1% -> 0% of each run, Pallas kernels for 0% -> 0%
where the time goes in v2:
time: 89.6 us; the launch traced here: 89.3 us
  Pallas kernels  80.9 us (90%)
  local copies, waits for them, and re-layouts  5.68 us (6%)
  other arithmetic  1.43 us (2%)
  between operations  1.29 us (1%)
    pallas_call x1, Pallas kernels, shards(): pl.pallas_call(body, out_shape=(jax.ShapeDtypeStruct((64, H), F32), jax.S...  80.9 us
    unnamed x3, local copies, waits for them, and re-layouts  4.99 us

profile of v2, /device:TPU:1, one launch (start us, length us, event | category | flops | bytes accessed | tf_op | source)
XLA Modules:
  0.0 89.3 jit_solution(12734373352217972416)
XLA Ops:
  1.3 0.7 broadcast_in_dim.27
  2.0 1.4 %pad_maximum_fusion.ramp_in = f32[26,288]{1,0:T(8,128)} fusion(f32[1,288]{1,0:T(1,128)S(1)} %broadcast_in_dim.27, f32[25,288]{1,0:T(8,128)} %param.19), kind=kLoop, calls=%fused_computation | loop fusion | flops 7488 | bytes 59904 | tf_op jit(solution)/shard_map/concatenate | solution.py:363
  3.4 80.9 %dispatch_window.1 = (f32[64,288]{1,0:T(8,128)}, f32[288,512]{1,0:T(8,128)}, f32[64,288]{1,0:T(8,128)}) custom-call(f32[64,288]{1,0:T(8,128)} %dispatch_in.1, f32[64,288]{1,0:T(8,128)} %bus_price_in.1, f32[1,64]{1,0:T(1,128)} %bitcast.15, f32[1,64]{1,0:T(1,128)} %bitcast.16, f32[1,64]{1,0:T(1,128)} %bitcast.17, s32[1,64]{1,0:T(1,128)} %bitcast.18, ...), custom_call_target="tpu_custom_call" | custom-call | tf_op jit(solution)/shard_map/dispatch_window/pallas_call | solution.py:391
  84.3 1.5 %copy.21 = f32[64,288]{1,0:T(8,128)} copy(f32[64,288]{1,0:T(8,128)} %get-tuple-element.12) | data formatting | bytes 147456
  85.9 1.9 %copy.22 = f32[512,288]{0,1:T(8,128)} copy(f32[512,288]{0,1:T(8,128)} %bitcast.14) | data formatting | bytes 1179648
  87.8 1.5 %copy.23 = f32[64,288]{1,0:T(8,128)} copy(f32[64,288]{1,0:T(8,128)} %get-tuple-element.14) | data formatting | bytes 147456

commit v3 on v2

--- a/solution.py
+++ b/solution.py
@@ -20,14 +20,14 @@
 
 
 def body(
-    dispatch_in, bus_price_in, marginal_in, quad_in, cap_in, width_in, bus_in, count_in, ramp_in,
+    dispatch_in, bus_price_in, marginal_in, quad_in, cap_in, width_in, bus_in, count_in, ramp_in, energy_in,
     load_in, ptdf_in, limit_in, lp_in,
     dispatch_out, line_out, bus_out,
-    dstage, pstage, prow, irow, crow, ramp_v, stage, xd, xp, rxd, rxp, pmo, rpm, pm, ids, ramp_t, kt, vb, dsp, px, oh,
+    dboth, pboth, prow, irow, crow, ramp_v, energy_v, stage, xd, xp, pm, ids, ramp_t, kt, vb, dsp, px, oh,
     pt, q, qt, ld, lim, lps, slim, slps, f0, f0full,
     ga, gb, fb, rc, sa, pb, rp,
-    halo_s, halo_p, halo_d, fin_s, fin_r, fd_s, fd_r, lr,
-    loc, ex_s, ex_r, id_s, id_r, q_s, q_r, ag_s, ag_r, zr_s, zr_r, zg_s, zg_r, rs_s, rs_r,
+    vbe, dse, halo_s, halo_p, halo_d, fin_s, fin_r, fd_s, fd_r, lr,
+    loc, ex_s, ex_r, cr_s, cr_r, id_s, id_r, q_s, q_r, ag_s, ag_r, zr_s, zr_r, zg_s, zg_r, rs_s, rs_r,
 ):
     z = lax.axis_index("region")
     p = lax.axis_index("plant")
@@ -36,6 +36,7 @@
     y = g % 4
     c = p % 2
     other = 1 - c
+    no = z // 8
 
     def dev(zz, gg, cc):
         return (zz, gg * 2 + cc)
@@ -70,9 +71,18 @@
     line_lane = pl.multiple_of(128 * (z % 4), 128)
     own_block = pl.ds(pl.multiple_of(512 * c, 512), 512)
     other_block = pl.ds(pl.multiple_of(512 * other, 512), 512)
-    small = [(bus_price_in, pstage), (marginal_in, prow.at[0:1]), (quad_in, prow.at[1:2]), (cap_in, prow.at[2:3]),
-             (width_in, irow.at[0:1]), (bus_in, irow.at[1:2]), (count_in, crow), (dispatch_in, dstage),
-             (ramp_in, ramp_v)]
+    own_lanes = pl.ds(pl.multiple_of(64 * c, 64), 64)
+    rows_in = [(marginal_in, 0), (quad_in, 1), (cap_in, 2)]
+    cores = [
+        (bus_price_in, pboth.at[own_lanes]),
+        *[(ref, prow.at[c, i:i + 1]) for ref, i in rows_in],
+        (width_in, irow.at[c, 0:1]), (bus_in, irow.at[c, 1:2]), (count_in, crow.at[c]),
+        (dispatch_in, dboth.at[own_lanes]),
+    ]
+    other_lanes = pl.ds(pl.multiple_of(64 * other, 64), 64)
+    cores_other = [pboth.at[other_lanes], *[prow.at[other, i:i + 1] for i in range(3)],
+                   irow.at[other, 0:1], irow.at[other, 1:2], crow.at[other], dboth.at[other_lanes]]
+    small = cores + [(ramp_in, ramp_v), (energy_in, energy_v)]
     large = [
         (load_in, ld),
         (ptdf_in, pt.at[own_block]),
@@ -90,28 +100,11 @@
     for peer in peers:
         pl.semaphore_signal(barrier, inc=1, device_id=peer, device_id_type=pl.DeviceIdType.MESH)
 
-    own_lanes = pl.ds(pl.multiple_of(64 * c, 64), 64)
     own_ext = pl.ds(pl.multiple_of(96 * c, 96), EXT)
-    other_ext = pl.ds(pl.multiple_of(96 * other, 96), EXT)
-    for copy in local[:len(small)]:
-        copy.wait()
-    stage[...] = jnp.zeros_like(stage)
-    stage[own_lanes, 0:H] = pstage[...]
-    xp[...] = stage[...].T
-    slot = lax.broadcasted_iota(jnp.int32, (1, 64), 1)
-    live_row = jnp.where(slot < crow[0:1, 0:1], 1.0, 0.0).astype(F32)
-    rows = jnp.concatenate(
-        [prow[...], irow[...].astype(F32), live_row, jnp.zeros((2, 64), F32)], axis=0)
-    gap = jnp.zeros_like(rows)
-    pmo[...] = jnp.where(
-        c == 0, jnp.concatenate([rows, gap], axis=1), jnp.concatenate([gap, rows], axis=1))
     pl.semaphore_wait(barrier, len(peers))
-    push(pmo, rpm, ex_s.at[1], ex_r.at[1], sibling)
-    push(xp.at[pl.ds(other_row, HALF)], rxp, ex_s.at[0], ex_r.at[0], sibling)
+    for i, (src, dst) in enumerate(cores):
+        push(src, dst, cr_s.at[i], cr_r.at[i], sibling)
     push(ptdf_in, pt.at[own_block], ex_s.at[3], ex_r.at[3], sibling)
-    stage[own_lanes, 0:H] = dstage[...]
-    xd[...] = stage[...].T
-    push(xd.at[other_ext], rxd, ex_s.at[2], ex_r.at[2], sibling)
     push(limit_in.at[pl.ds(other_row, HALF), pl.ds(line_lane, 128)], slim, ex_s.at[4], ex_r.at[4], sibling)
     push(lp_in.at[pl.ds(other_row, HALF), pl.ds(line_lane, 128)], slps, ex_s.at[5], ex_r.at[5], sibling)
 
@@ -123,16 +116,25 @@
         arrived(grid.at[s, pl.ds(0, 15)], ag_r.at[k, s])
         return jnp.concatenate([grid[s, i] for i in range(16)], axis=1)
 
-    arrived(rpm, ex_r.at[1])
-    pm[...] = pmo[...] + rpm[...]
+    for copy in local[:len(small)]:
+        copy.wait()
+    for i in range(1, 7):
+        arrived(cores_other[i], cr_r.at[i])
+    slot = lax.broadcasted_iota(jnp.int32, (1, 64), 1)
+    pm[...] = jnp.concatenate([
+        jnp.concatenate([
+            prow[i], irow[i].astype(F32), jnp.where(slot < crow[i], 1.0, 0.0).astype(F32),
+            jnp.zeros((2, 64), F32),
+        ], axis=0) for i in (0, 1)], axis=1)
     ids[g] = pm[...]
     for d in others:
         push(ids.at[g], ids.at[g], id_s.at[0], id_r.at[0], dev(z, chip(*d), c))
-    arrived(rxp, ex_r.at[0])
-    for s in range(PARTS):
-        row = offset(s, c)
-        mine = xp[pl.ds(pl.multiple_of(own_row + row, 16), PART)]
-        ga[s, g] = (mine + rxp[pl.ds(row, PART)]).astype(BF16)
+    arrived(cores_other[0], cr_r.at[0])
+    stage[...] = jnp.zeros_like(stage)
+    stage[:, 0:H] = pboth[...]
+    xp[...] = stage[...].T
+    for s in range(PARTS):
+        ga[s, g] = xp[pl.ds(pl.multiple_of(own_row + offset(s, c), 16), PART)].astype(BF16)
         gather(ga, s, 0)
 
     for copy in local[len(small):]:
@@ -146,7 +148,8 @@
     push(f0full.at[:, pl.ds(other_row, HALF)], f0.at[own_pairs], ex_s.at[11], ex_r.at[11], sibling)
 
     stage[...] = jnp.zeros_like(stage)
-    stage[0:26, 0:H] = ramp_v[...]
+    stage[0:25, 0:H] = ramp_v[...]
+    stage[25:26, 0:H] = energy_v[...].reshape(1, H)
     ramp_t[...] = stage[...].T
     marginal, quad, cap, width = (pm[i:i + 1] for i in range(4))
     live = pm[5:6]
@@ -183,25 +186,16 @@
     def price_part(s):
         px[ext_part(s)] = jnp.dot(gathered(ga, s, 0), oh[...], preferred_element_type=F32)
 
+    vb[...] = jnp.zeros_like(vb)
+    vbe[...] = jnp.zeros_like(vbe)
     lax.fori_loop(0, 2, plant_columns, 0)
     price_part(0)
     halo_s[0] = px[ext_part(0)]
     push(halo_s.at[0], halo_p.at[0], ex_s.at[6], ex_r.at[6], sibling)
-    arrived(rxd, ex_r.at[2])
-    dsp[...] = xd[own_ext] + rxd[...]
-    lax.fori_loop(2, 4, plant_columns, 0)
-    price_part(1)
-    arrived(slim, ex_r.at[4])
-    arrived(slps, ex_r.at[5])
-    holds = c == z // 4
-    lim[...] = jnp.where(holds, lim[...], slim[...])
-    lps[...] = jnp.where(holds, lps[...], slps[...])
-    arrived(f0.at[pl.ds(2 * other, 2)], ex_r.at[11])
-    vb[...] = jnp.zeros_like(vb)
-    arrived(halo_p.at[0], ex_r.at[6])
-    px[pl.ds(halo_at, PART)] = halo_p[0]
-    price_part(2)
-
+    arrived(cores_other[7], cr_r.at[7])
+    stage[:, 0:H] = dboth[...]
+    xd[...] = stage[...].T
+    dsp[...] = xd[own_ext]
     def sweep(_, carry):
         d = dsp[...]
         vb[16:16 + EXT] = d + 0.5 * (px[...] - marginal - quad * d)
@@ -213,8 +207,31 @@
             dsp[r:r + 64] = live * jnp.clip(total, 0.0, cap)
         return carry
 
-    def start_gather(k):
-        for s in range(PARTS):
+    early_row = pl.multiple_of(48 * other, 16)
+
+    def early_part(k):
+        rows = pl.ds(early_row, HALF)
+        price = px[rows]
+        dse[...] = dsp[rows]
+
+        def step(_, carry):
+            d = dse[...]
+            vbe[16:16 + HALF] = d + 0.5 * (price - marginal - quad * d)
+            for r in range(0, HALF, PART):
+                at = pl.ds(pl.multiple_of(early_row + r, 16), PART)
+                total = kt[REACH, at] * vbe[16 + r:16 + r + PART]
+                for s in range(1, REACH + 1):
+                    for o in (s, -s):
+                        total = total + kt[REACH + o, at] * vbe[16 + o + r:16 + o + r + PART]
+                dse[r:r + PART] = live * jnp.clip(total, 0.0, cap)
+            return carry
+
+        lax.fori_loop(0, ITERS, step, 0)
+        gb[k, 0, g] = dse[PART:2 * PART].astype(BF16)
+        gather(gb.at[k], 0, 1 + k)
+
+    def other_parts(k):
+        for s in range(1, PARTS):
             gb[k, s, g] = dsp[ext_part(s)].astype(BF16)
             gather(gb.at[k], s, 1 + k)
 
@@ -272,37 +289,53 @@
         row = pl.multiple_of(own_row + offset(s, c), 16)
         return ramp_t[pl.ds(row, PART), 25:26] - total
 
+    lax.fori_loop(2, 3 + no, plant_columns, 0)
+    price_part(1)
+    arrived(halo_p.at[0], ex_r.at[6])
+    px[pl.ds(halo_at, PART)] = halo_p[0]
+    early_part(0)
+    price_part(2)
     lax.fori_loop(0, ITERS, sweep, 0)
-    start_gather(0)
+    other_parts(0)
     halo_s[1] = dsp[ext_part(0)]
     push(halo_s.at[1], halo_d, ex_s.at[7], ex_r.at[7], sibling)
+    lax.fori_loop(3, 4 + no, plant_columns, 0)
+    arrived(slim, ex_r.at[4])
+    arrived(slps, ex_r.at[5])
+    holds = c == z // 4
+    lim[...] = jnp.where(holds, lim[...], slim[...])
+    lps[...] = jnp.where(holds, lps[...], slps[...])
+    arrived(f0.at[pl.ds(2 * other, 2)], ex_r.at[11])
+
+    def transpose_columns(j, core):
+        i = 4 * core + j
+        for pair in range(4):
+            qt[pair, pl.ds(pl.multiple_of(256 * i, 256), 256)] = q[i, 256 * pair:256 * pair + 256].T
+        return core
+
+    lax.fori_loop(0, 4, transpose_columns, c)
     for j in range(4):
         arrived(q.at[4 * other + j], q_r.at[j])
-
-    def transpose_columns(i, _):
-        for pair in range(4):
-            qt[pair, pl.ds(pl.multiple_of(256 * i, 256), 256)] = q[i, 256 * pair:256 * pair + 256].T
-        return 0
-
-    lax.fori_loop(0, 8, transpose_columns, 0)
+    lax.fori_loop(0, 4, transpose_columns, other)
     for s in range(PARTS):
         flow(0, s)
     for s in range(PARTS):
         limit_lines(0, s)
     for s in range(PARTS):
         congestion(0, s)
-    for s in range(PARTS):
-        px[ext_part(s)] = prices(0, s)
-        if s == 0:
-            halo_s[2] = px[ext_part(0)]
-            push(halo_s.at[2], halo_p.at[1], ex_s.at[8], ex_r.at[8], sibling)
-            arrived(halo_d, ex_r.at[7])
-            dsp[pl.ds(halo_at, PART)] = halo_d[...]
+    px[ext_part(0)] = prices(0, 0)
+    halo_s[2] = px[ext_part(0)]
+    push(halo_s.at[2], halo_p.at[1], ex_s.at[8], ex_r.at[8], sibling)
+    arrived(halo_d, ex_r.at[7])
+    dsp[pl.ds(halo_at, PART)] = halo_d[...]
+    px[ext_part(1)] = prices(0, 1)
     arrived(halo_p.at[1], ex_r.at[8])
     px[pl.ds(halo_at, PART)] = halo_p[1]
 
+    early_part(1)
+    px[ext_part(2)] = prices(0, 2)
     lax.fori_loop(0, ITERS, sweep, 0)
-    start_gather(1)
+    other_parts(1)
     fd_s[...] = dsp[pl.ds(core_row, HALF)]
     push(fd_s, fd_r, ex_s.at[9], ex_r.at[9], sibling)
 
@@ -340,7 +373,9 @@
     stage[...] = rows_out(fin_s[...], fin_r[...])
     bus_out[...] = stage[own_lanes, 0:H]
 
-    for ref, i in ((pmo, 1), (rxp, 0), (ptdf_in, 3), (rxd, 2), (slim, 4), (slps, 5), (f0.at[own_pairs], 11),
+    for i, (ref, _) in enumerate(cores):
+        sent_off(ref, cr_s.at[i])
+    for ref, i in ((ptdf_in, 3), (slim, 4), (slps, 5), (f0.at[own_pairs], 11),
                    (halo_s.at[0], 6), (halo_s.at[1], 7), (halo_s.at[2], 8), (fd_s, 9), (lr, 10),
                    (fin_s.at[0:PART], 12), (fin_s.at[0:PART], 13), (fin_s.at[0:PART], 14)):
         sent_off(ref, ex_s.at[i])
@@ -360,18 +395,19 @@
     dispatch_start, marginal_cost, quad_cost, capacity, band_widths, ramp_band, plant_bus, plant_counts,
     load, ptdf, line_limit, line_price_start, bus_price_start, energy_price,
 ):
-    ramp = jnp.concatenate([ramp_band, energy_price[None]], axis=0)
     vmem = pl.BlockSpec(memory_space=pltpu.VMEM)
     hbm = pl.BlockSpec(memory_space=pltpu.HBM)
     sem = pltpu.SemaphoreType.DMA
 
+    def in_hbm(array):
+        return pltpu.with_memory_space_constraint(array, pltpu.HBM)
+
     def v(shape, kind=F32):
         return pltpu.VMEM(shape, kind)
 
     scratch = [
-        v((64, H)), v((64, H)), v((3, 64)), v((2, 64), jnp.int32), v((1, 1), jnp.int32), v((26, H)),
-        v((128, 384)), v((384, 128)), v((384, 128)), v((EXT, 128)), v((HALF, 128)),
-        v((8, 128)), v((8, 128)), v((8, 128)), v((16, 8, 128)),
+        v((128, H)), v((128, H)), v((2, 3, 64)), v((2, 2, 64), jnp.int32), v((2, 1, 1), jnp.int32), v((25, H)), v((H,)),
+        v((128, 384)), v((384, 128)), v((384, 128)), v((8, 128)), v((16, 8, 128)),
         v((384, 128)), v((25, EXT, 128)), v((EXT + 32, 128)), v((EXT, 128)), v((EXT, 128)),
         v((2048, 128), BF16),
         v((1024, 2048), BF16), v((8, 1024, 256), BF16), v((4, 2048, 256), BF16), v((H, 2048)),
@@ -381,10 +417,11 @@
         v((2, PARTS, 8, PART, 128), BF16), v((2, PARTS, 8, PART, 128), BF16),
         v((2, PARTS, 8, PART, 128), BF16),
         v((2, PARTS, 16, PART, 128), BF16), v((2, PARTS, 16, PART, 128), BF16),
+        v((HALF + 32, 128)), v((HALF, 128)),
         v((3, PART, 128)), v((2, PART, 128)), v((PART, 128)),
         v((HALF, 128)), v((HALF, 128)), v((HALF, 128)), v((HALF, 128)),
         v((PARTS, 4, PART, 128), BF16),
-        sem((13,)), sem((15,)), sem((15,)), sem((1,)), sem((1,)), sem((4,)), sem((4,)),
+        sem((14,)), sem((15,)), sem((15,)), sem((8,)), sem((8,)), sem((1,)), sem((1,)), sem((4,)), sem((4,)),
         sem((3, PARTS)), sem((3, PARTS)), sem((2, PARTS)), sem((2, PARTS)), sem((2, PARTS)), sem((2, PARTS)),
         sem((2, PARTS)), sem((2, PARTS)),
     ]
@@ -395,16 +432,17 @@
             jax.ShapeDtypeStruct((H, 512), F32),
             jax.ShapeDtypeStruct((64, H), F32),
         ),
-        in_specs=[hbm] * 13,
+        in_specs=[hbm] * 14,
         out_specs=(vmem,) * 3,
         scratch_shapes=scratch,
         compiler_params=pltpu.CompilerParams(
-            collective_id=0, has_side_effects=True, vmem_limit_bytes=56 * 2**20),
+            collective_id=0, has_side_effects=True, vmem_limit_bytes=40 * 2**20),
         name="dispatch_window",
     )(
-        dispatch_start, bus_price_start, marginal_cost[None], quad_cost[None], capacity[None],
-        band_widths[None], plant_bus[None], plant_counts[None], ramp, load.T, ptdf, line_limit.T,
-        line_price_start.T,
+        *map(in_hbm, (dispatch_start, bus_price_start, marginal_cost[None], quad_cost[None], capacity[None],
+                      band_widths[None], plant_bus[None])),
+        plant_counts[None],
+        *map(in_hbm, (ramp_band, energy_price, load.T, ptdf, line_limit.T, line_price_start.T)),
     )
     return dispatch, line_price.T, bus_price
 

time: 89.6 us -> 82 us (0.915)
  local copies, waits for them, and re-layouts: 5.68 us -> 2.1 us
  Pallas kernels: 80.9 us -> 78.5 us
  other arithmetic: 1.43 us -> 0 us
    unnamed x3, local copies, waits for them, and re-layouts: 4.99 us -> 2.1 us
    pallas_call x1, Pallas kernels: 80.9 us -> 78.5 us  [shards(): pl.pallas_call(body, out_shape=(jax.ShapeDtypeStruct((64, H), F32), jax.S...]
    concatenate x1 -> x0, other arithmetic: 1.43 us -> none  [shards(): ramp = jnp.concatenate([ramp_band, energy_price[None]], axis=0)]
where the time goes in v3:
time: 82 us; the launch traced here: 81.9 us
  Pallas kernels  78.5 us (96%)
  local copies, waits for them, and re-layouts  2.1 us (3%)
  between operations  1.29 us (2%)
    pallas_call x1, Pallas kernels, shards(): pl.pallas_call(body, out_shape=(jax.ShapeDtypeStruct((64, H), F32), jax.S...  78.5 us
    unnamed x3, local copies, waits for them, and re-layouts  2.1 us

profile of v3, /device:TPU:1, one launch (start us, length us, event | category | flops | bytes accessed | tf_op | source)
XLA Modules:
  0.0 81.9 jit_solution(6904716684298754385)
XLA Ops:
  1.3 78.5 %dispatch_window.1 = (f32[64,288]{1,0:T(8,128)S(1)}, f32[288,512]{1,0:T(8,128)S(1)}, f32[64,288]{1,0:T(8,128)S(1)}) custom-call(f32[64,288]{1,0:T(8,128)} %dispatch_in.1, f32[64,288]{1,0:T(8,128)} %bus_price_in.1, f32[1,64]{1,0:T(1,128)} %bitcast.15, f32[1,64]{1,0:T(1,128)} %bitcast.16, f32[1,64]{1,0:T(1,128)} %bitcast.17, s32[1,64]{1,0:T(1,128)} %bitcast.18, ...), custom_call_target="tpu_custom_call" | custom-call | tf_op jit(solution)/shard_map/dispatch_window/pallas_call | solution.py:428
  79.8 0.6 copy.21
  80.4 0.8 copy.22
  81.3 0.6 copy.23

commit v4 on v3

--- a/solution.py
+++ b/solution.py
@@ -8,8 +8,11 @@
 H = 288
 HALF = 144
 EXT = 192
-PARTS = 3
-PART = 48
+SIZES = (48, 48, 48)
+STARTS = (0, 48, 96)
+PARTS = len(SIZES)
+MOST = max(SIZES)
+HALO = 48
 REACH = 12
 ITERS = 3
 F32 = jnp.float32
@@ -22,12 +25,12 @@
 def body(
     dispatch_in, bus_price_in, marginal_in, quad_in, cap_in, width_in, bus_in, count_in, ramp_in, energy_in,
     load_in, ptdf_in, limit_in, lp_in,
-    dispatch_out, line_out, bus_out,
+    both_out, line_out,
     dboth, pboth, prow, irow, crow, ramp_v, energy_v, stage, xd, xp, pm, ids, ramp_t, kt, vb, dsp, px, oh,
     pt, q, qt, ld, lim, lps, slim, slps, f0, f0full,
     ga, gb, fb, rc, sa, pb, rp,
     vbe, dse, halo_s, halo_p, halo_d, fin_s, fin_r, fd_s, fd_r, lr,
-    loc, ex_s, ex_r, cr_s, cr_r, id_s, id_r, q_s, q_r, ag_s, ag_r, zr_s, zr_r, zg_s, zg_r, rs_s, rs_r,
+    loc, ex_s, ex_r, lr_s, lr_r, fin_ss, fin_rs, cr_s, cr_r, id_s, id_r, q_s, q_r, ag_s, ag_r, zr_s, zr_r, zg_s, zg_r, rs_s, rs_r,
 ):
     z = lax.axis_index("region")
     p = lax.axis_index("plant")
@@ -46,7 +49,7 @@
     def chip(dx, dy):
         return ((x + dx) % 4) * 4 + (y + dy) % 4
 
-    others = [(dx, dy) for dx in (2, 1, 3, 0) for dy in (2, 1, 3, 0) if dx or dy]
+    others = [(dx, dy) for dy in (2, 1, 3, 0) for dx in (2, 1, 3, 0) if dx or dy]
 
     def remote(src, dst, send, recv, device):
         return pltpu.make_async_remote_copy(
@@ -64,7 +67,7 @@
         remote(src, src, send, ex_r.at[0], sibling).wait_send()
 
     def offset(s, core):
-        return pl.multiple_of(core * PART * s + (1 - core) * (HALF - PART - PART * s), 16)
+        return pl.multiple_of(core * STARTS[s] + (1 - core) * (HALF - STARTS[s] - SIZES[s]), 16)
 
     own_row = pl.multiple_of(HALF * c, 16)
     other_row = pl.multiple_of(HALF * other, 16)
@@ -95,7 +98,7 @@
 
     barrier = pltpu.get_barrier_semaphore()
     peers = [sibling]
-    peers += [dev(z, chip(*d), c) for d in others]
+    peers += [dev(z, chip(*d), core) for d in others for core in (c, other)]
     peers += [dev((z + d) % 8, g, c) for d in range(1, 8)]
     for peer in peers:
         pl.semaphore_signal(barrier, inc=1, device_id=peer, device_id_type=pl.DeviceIdType.MESH)
@@ -104,17 +107,21 @@
     pl.semaphore_wait(barrier, len(peers))
     for i, (src, dst) in enumerate(cores):
         push(src, dst, cr_s.at[i], cr_r.at[i], sibling)
+    for d in others:
+        for core in (c, other):
+            push(bus_in, ids.at[g, c], id_s.at[0], id_r.at[0], dev(z, chip(*d), core))
     push(ptdf_in, pt.at[own_block], ex_s.at[3], ex_r.at[3], sibling)
     push(limit_in.at[pl.ds(other_row, HALF), pl.ds(line_lane, 128)], slim, ex_s.at[4], ex_r.at[4], sibling)
     push(lp_in.at[pl.ds(other_row, HALF), pl.ds(line_lane, 128)], slps, ex_s.at[5], ex_r.at[5], sibling)
 
     def gather(grid, s, k):
         for d in others:
-            push(grid.at[s, g], grid.at[s, g], ag_s.at[k, s], ag_r.at[k, s], dev(z, chip(*d), c))
+            block = grid.at[s, g, pl.ds(0, SIZES[s])]
+            push(block, block, ag_s.at[k, s], ag_r.at[k, s], dev(z, chip(*d), c))
 
     def gathered(grid, s, k):
-        arrived(grid.at[s, pl.ds(0, 15)], ag_r.at[k, s])
-        return jnp.concatenate([grid[s, i] for i in range(16)], axis=1)
+        arrived(grid.at[s, pl.ds(0, 15), pl.ds(0, SIZES[s])], ag_r.at[k, s])
+        return jnp.concatenate([grid[s, i, 0:SIZES[s]] for i in range(16)], axis=1)
 
     for copy in local[:len(small)]:
         copy.wait()
@@ -126,15 +133,14 @@
             prow[i], irow[i].astype(F32), jnp.where(slot < crow[i], 1.0, 0.0).astype(F32),
             jnp.zeros((2, 64), F32),
         ], axis=0) for i in (0, 1)], axis=1)
-    ids[g] = pm[...]
-    for d in others:
-        push(ids.at[g], ids.at[g], id_s.at[0], id_r.at[0], dev(z, chip(*d), c))
+    for i in (0, 1):
+        ids[g, i] = irow[i, 1:2]
     arrived(cores_other[0], cr_r.at[0])
     stage[...] = jnp.zeros_like(stage)
     stage[:, 0:H] = pboth[...]
     xp[...] = stage[...].T
     for s in range(PARTS):
-        ga[s, g] = xp[pl.ds(pl.multiple_of(own_row + offset(s, c), 16), PART)].astype(BF16)
+        ga[s, g, 0:SIZES[s]] = xp[pl.ds(pl.multiple_of(own_row + offset(s, c), 16), SIZES[s])].astype(BF16)
         gather(ga, s, 0)
 
     for copy in local[len(small):]:
@@ -170,9 +176,9 @@
 
     def plant_columns(j, _):
         i = 4 * c + j
-        bus = jnp.concatenate([ids[2 * i, 4:5], ids[2 * i + 1, 4:5]], axis=1)
+        bus = jnp.concatenate([ids[2 * i + a, b] for a in (0, 1) for b in (0, 1)], axis=1)
         iota = lax.broadcasted_iota(jnp.int32, (2048, 256), 0)
-        one_hot = jnp.where(iota == bus.astype(jnp.int32), 1.0, 0.0).astype(BF16)
+        one_hot = jnp.where(iota == bus, 1.0, 0.0).astype(BF16)
         q[i] = jnp.dot(pt[...], one_hot, preferred_element_type=F32).astype(BF16)
         push(q.at[i], q.at[i], q_s.at[j], q_r.at[j], sibling)
         return 0
@@ -181,7 +187,7 @@
     halo_at = pl.multiple_of(HALF * other, 16)
 
     def ext_part(s):
-        return pl.ds(pl.multiple_of(core_row + offset(s, c), 16), PART)
+        return pl.ds(pl.multiple_of(core_row + offset(s, c), 16), SIZES[s])
 
     def price_part(s):
         px[ext_part(s)] = jnp.dot(gathered(ga, s, 0), oh[...], preferred_element_type=F32)
@@ -214,87 +220,102 @@
         price = px[rows]
         dse[...] = dsp[rows]
 
-        def step(_, carry):
-            d = dse[...]
-            vbe[16:16 + HALF] = d + 0.5 * (price - marginal - quad * d)
-            for r in range(0, HALF, PART):
-                at = pl.ds(pl.multiple_of(early_row + r, 16), PART)
-                total = kt[REACH, at] * vbe[16 + r:16 + r + PART]
+        first, last = 0, HALF
+        for low, high in ((24, 120), (32, 112), (48, 96)):
+            d = dse[first:last]
+            vbe[16 + first:16 + last] = d + 0.5 * (price[first:last] - marginal - quad * d)
+            for r in range(low, high, 48 if high - low == 96 else (high - low) // 2):
+                size = 48 if high - low == 96 else (high - low) // 2
+                at = pl.ds(pl.multiple_of(early_row + r, 8), size)
+                total = kt[REACH, at] * vbe[16 + r:16 + r + size]
                 for s in range(1, REACH + 1):
                     for o in (s, -s):
-                        total = total + kt[REACH + o, at] * vbe[16 + o + r:16 + o + r + PART]
-                dse[r:r + PART] = live * jnp.clip(total, 0.0, cap)
-            return carry
-
-        lax.fori_loop(0, ITERS, step, 0)
-        gb[k, 0, g] = dse[PART:2 * PART].astype(BF16)
+                        total = total + kt[REACH + o, at] * vbe[16 + o + r:16 + o + r + size]
+                dse[r:r + size] = live * jnp.clip(total, 0.0, cap)
+            first, last = low, high
+
+        gb[k, 0, g, 0:HALO] = dse[HALO:2 * HALO].astype(BF16)
         gather(gb.at[k], 0, 1 + k)
 
     def other_parts(k):
         for s in range(1, PARTS):
-            gb[k, s, g] = dsp[ext_part(s)].astype(BF16)
+            gb[k, s, g, 0:SIZES[s]] = dsp[ext_part(s)].astype(BF16)
             gather(gb.at[k], s, 1 + k)
 
     def flow(k, s):
         spread = gathered(gb.at[k], s, 1 + k)
-        rows = pl.ds(offset(s, c), PART)
-        for dq in (2, 1, 3, 0):
-            pair = (z // 2 + dq) % 4
+        n = SIZES[s]
+        rows = pl.ds(offset(s, c), n)
+        for pair in range(4):
             part = jnp.dot(spread, qt[pair], preferred_element_type=F32) - f0[pair, rows]
             for j in (0, 1):
-                fb[k, s, 2 * pair + j] = part[:, 128 * j:128 * j + 128].astype(BF16)
-            for j in (0, 1):
-                target = 2 * pair + j
-
-                @pl.when(target != z)
-                def _():
-                    push(fb.at[k, s, target], rc.at[k, s, z], zr_s.at[k, s], zr_r.at[k, s], dev(target, g, c))
+                fb[k, s, 2 * pair + j, 0:n] = part[:, 128 * j:128 * j + 128].astype(BF16)
+        for d in (4, 3, 5, 2, 6, 1, 7):
+            target = (z + d) % 8
+            push(fb.at[k, s, target, pl.ds(0, n)], rc.at[k, s, z, pl.ds(0, n)], zr_s.at[k, s],
+                 zr_r.at[k, s], dev(target, g, c))
 
     def limit_lines(k, s):
-        arrived(rc.at[k, s, pl.ds(0, 7)], zr_r.at[k, s])
-        total = fb[k, s, z].astype(F32)
+        n = SIZES[s]
+        arrived(rc.at[k, s, pl.ds(0, 7), pl.ds(0, n)], zr_r.at[k, s])
+        total = fb[k, s, z, 0:n].astype(F32)
         for d in range(1, 8):
-            total = total + rc[k, s, (z + d) % 8].astype(F32)
-        rows = pl.ds(offset(s, c), PART)
+            total = total + rc[k, s, (z + d) % 8, 0:n].astype(F32)
+        rows = pl.ds(offset(s, c), n)
         shifted = lps[rows] + total
         limit = lim[rows]
         new = shifted - jnp.clip(shifted, -limit, limit)
         lps[rows] = new
-        sa[k, s, z] = new.astype(BF16)
+        sa[k, s, z, 0:n] = new.astype(BF16)
+        block = sa.at[k, s, z, pl.ds(0, n)]
         for d in (4, 3, 5, 2, 6, 1, 7):
-            push(sa.at[k, s, z], sa.at[k, s, z], zg_s.at[k, s], zg_r.at[k, s], dev((z + d) % 8, g, c))
+            push(block, block, zg_s.at[k, s], zg_r.at[k, s], dev((z + d) % 8, g, c))
 
     def congestion(k, s):
-        arrived(sa.at[k, s, pl.ds(0, 7)], zg_r.at[k, s])
-        spread = jnp.concatenate([sa[k, s, i] for i in range(8)], axis=1)
-        for dx in (2, 1, 3, 0):
-            row = (x + dx) % 4
-            for h in (0, 1):
-                i = 2 * row + h
-                matrix = q[i] if k == 0 else pt[:, pl.ds(pl.multiple_of(256 * i, 256), 256)]
-                part = jnp.dot(spread, matrix, preferred_element_type=F32).astype(BF16)
-                pb[k, s, 2 * i] = part[:, 0:128]
-                pb[k, s, 2 * i + 1] = part[:, 128:256]
-            for dy in (2, 1, 3, 0):
-                if dx or dy:
-                    to = chip(dx, dy)
-                    push(pb.at[k, s, to], rp.at[k, s, g], rs_s.at[k, s], rs_r.at[k, s], dev(z, to, c))
-
+        n = SIZES[s]
+        arrived(sa.at[k, s, pl.ds(0, 7), pl.ds(0, n)], zg_r.at[k, s])
+        spread = jnp.concatenate([sa[k, s, i, 0:n] for i in range(8)], axis=1)
+        for i in range(8):
+            matrix = q[i] if k == 0 else pt[:, 256 * i:256 * i + 256]
+            part = jnp.dot(spread, matrix, preferred_element_type=F32).astype(BF16)
+            pb[k, s, 2 * i, 0:n] = part[:, 0:128]
+            pb[k, s, 2 * i + 1, 0:n] = part[:, 128:256]
+        for dx, dy in others:
+            to = chip(dx, dy)
+            push(pb.at[k, s, to, pl.ds(0, n)], rp.at[k, s, g, pl.ds(0, n)], rs_s.at[k, s], rs_r.at[k, s],
+                 dev(z, to, c))
 
     def prices(k, s):
-        arrived(rp.at[k, s, pl.ds(0, 15)], rs_r.at[k, s])
-        total = pb[k, s, g].astype(F32)
+        n = SIZES[s]
+        arrived(rp.at[k, s, pl.ds(0, 15), pl.ds(0, n)], rs_r.at[k, s])
+        total = pb[k, s, g, 0:n].astype(F32)
         for d in range(1, 16):
-            total = total + rp[k, s, (g + d) % 16].astype(F32)
+            total = total + rp[k, s, (g + d) % 16, 0:n].astype(F32)
         row = pl.multiple_of(own_row + offset(s, c), 16)
-        return ramp_t[pl.ds(row, PART), 25:26] - total
+        return ramp_t[pl.ds(row, n), 25:26] - total
+
+    def drain(steps, refs):
+        for ref, i in refs:
+            sent_off(ref, ex_s.at[i])
+        for s in range(PARTS):
+            rows = pl.ds(0, SIZES[s])
+            for k in (0, 1) if 0 in steps else (2,):
+                sent_off(ga.at[s, pl.ds(0, 15), rows], ag_s.at[k, s])
+            for k in steps:
+                sent_off(rc.at[k, s, pl.ds(0, 7), rows], zr_s.at[k, s])
+                sent_off(sa.at[k, s, pl.ds(0, 7), rows], zg_s.at[k, s])
+                sent_off(rp.at[k, s, pl.ds(0, 15), rows], rs_s.at[k, s])
+            if 1 in steps:
+                sent_off(fin_s.at[rows], fin_ss.at[s])
+                sent_off(lr.at[s, :, rows], lr_s.at[s])
 
     lax.fori_loop(2, 3 + no, plant_columns, 0)
     price_part(1)
     arrived(halo_p.at[0], ex_r.at[6])
-    px[pl.ds(halo_at, PART)] = halo_p[0]
+    px[pl.ds(halo_at, HALO)] = halo_p[0]
     early_part(0)
-    price_part(2)
+    for s in range(2, PARTS):
+        price_part(s)
     lax.fori_loop(0, ITERS, sweep, 0)
     other_parts(0)
     halo_s[1] = dsp[ext_part(0)]
@@ -327,13 +348,14 @@
     halo_s[2] = px[ext_part(0)]
     push(halo_s.at[2], halo_p.at[1], ex_s.at[8], ex_r.at[8], sibling)
     arrived(halo_d, ex_r.at[7])
-    dsp[pl.ds(halo_at, PART)] = halo_d[...]
+    dsp[pl.ds(halo_at, HALO)] = halo_d[...]
     px[ext_part(1)] = prices(0, 1)
     arrived(halo_p.at[1], ex_r.at[8])
-    px[pl.ds(halo_at, PART)] = halo_p[1]
+    px[pl.ds(halo_at, HALO)] = halo_p[1]
 
     early_part(1)
-    px[ext_part(2)] = prices(0, 2)
+    for s in range(2, PARTS):
+        px[ext_part(s)] = prices(0, s)
     lax.fori_loop(0, ITERS, sweep, 0)
     other_parts(1)
     fd_s[...] = dsp[pl.ds(core_row, HALF)]
@@ -347,48 +369,42 @@
 
     arrived(fd_r, ex_r.at[9])
     stage[...] = rows_out(fd_s[...], fd_r[...])
-    dispatch_out[...] = stage[own_lanes, 0:H]
-    for s in range(PARTS):
-        flow(1, s)
-    for s in range(PARTS):
-        limit_lines(1, s)
-    for s in range(PARTS):
-        congestion(1, s)
-    push(sa.at[1, :, pl.ds(pl.multiple_of(4 * other, 4), 4)], lr, ex_s.at[10], ex_r.at[10], sibling)
-    for s in range(PARTS):
-        rows = pl.ds(pl.multiple_of(own_row + offset(s, c), 16), PART)
-        for i in range(4):
-            line_out[rows, 128 * i:128 * i + 128] = sa[1, s, 4 * c + i].astype(F32)
-    for s in range(PARTS):
-        rows = pl.ds(offset(s, c), PART)
-        fin_s[rows] = prices(1, s)
-        push(fin_s.at[rows], fin_r.at[rows], ex_s.at[12 + s], ex_r.at[12 + s], sibling)
-    arrived(lr, ex_r.at[10])
-    for s in range(PARTS):
-        rows = pl.ds(pl.multiple_of(other_row + offset(s, other), 16), PART)
-        for i in range(4):
-            line_out[rows, 128 * i:128 * i + 128] = lr[s, i].astype(F32)
-    for s in range(PARTS):
-        arrived(fin_r.at[pl.ds(offset(s, other), PART)], ex_r.at[12 + s])
-    stage[...] = rows_out(fin_s[...], fin_r[...])
-    bus_out[...] = stage[own_lanes, 0:H]
-
+    both_out[0] = stage[own_lanes, 0:H]
     for i, (ref, _) in enumerate(cores):
         sent_off(ref, cr_s.at[i])
-    for ref, i in ((ptdf_in, 3), (slim, 4), (slps, 5), (f0.at[own_pairs], 11),
-                   (halo_s.at[0], 6), (halo_s.at[1], 7), (halo_s.at[2], 8), (fd_s, 9), (lr, 10),
-                   (fin_s.at[0:PART], 12), (fin_s.at[0:PART], 13), (fin_s.at[0:PART], 14)):
-        sent_off(ref, ex_s.at[i])
     sent_off(ids.at[pl.ds(0, 15)], id_s.at[0])
     for j in range(4):
         sent_off(q.at[j], q_s.at[j])
-    for s in range(PARTS):
-        for k in range(3):
-            sent_off(ga.at[s, pl.ds(0, 15), pl.ds(0, PART)], ag_s.at[k, s])
-        for k in range(2):
-            sent_off(rc.at[k, s, pl.ds(0, 7)], zr_s.at[k, s])
-            sent_off(sa.at[k, s, pl.ds(0, 7)], zg_s.at[k, s])
-            sent_off(rp.at[k, s, pl.ds(0, 15)], rs_s.at[k, s])
+    drain((0,), ((ptdf_in, 3), (slim, 4), (slps, 5), (f0.at[own_pairs], 11), (halo_s.at[0], 6), (halo_s.at[1], 7),
+                 (halo_s.at[2], 8)))
+    for s in range(PARTS):
+        flow(1, s)
+    for s in range(PARTS):
+        limit_lines(1, s)
+    for s in range(PARTS):
+        congestion(1, s)
+    for s in range(PARTS):
+        push(sa.at[1, s, pl.ds(4 * other, 4), pl.ds(0, SIZES[s])], lr.at[s, :, pl.ds(0, SIZES[s])], lr_s.at[s],
+             lr_r.at[s], sibling)
+    for s in range(PARTS):
+        rows = pl.ds(pl.multiple_of(own_row + offset(s, c), 16), SIZES[s])
+        for i in range(4):
+            line_out[rows, 128 * i:128 * i + 128] = sa[1, s, 4 * c + i, 0:SIZES[s]].astype(F32)
+    for s in range(PARTS):
+        rows = pl.ds(offset(s, c), SIZES[s])
+        fin_s[rows] = prices(1, s)
+        push(fin_s.at[rows], fin_r.at[rows], fin_ss.at[s], fin_rs.at[s], sibling)
+    for s in range(PARTS):
+        arrived(lr.at[s, :, pl.ds(0, SIZES[s])], lr_r.at[s])
+        rows = pl.ds(pl.multiple_of(other_row + offset(s, other), 16), SIZES[s])
+        for i in range(4):
+            line_out[rows, 128 * i:128 * i + 128] = lr[s, i, 0:SIZES[s]].astype(F32)
+    for s in range(PARTS):
+        arrived(fin_r.at[pl.ds(offset(s, other), SIZES[s])], fin_rs.at[s])
+    stage[...] = rows_out(fin_s[...], fin_r[...])
+    both_out[1] = stage[own_lanes, 0:H]
+
+    drain((1,), ((fd_s, 9),))
 
 
 def shards(
@@ -407,33 +423,32 @@
 
     scratch = [
         v((128, H)), v((128, H)), v((2, 3, 64)), v((2, 2, 64), jnp.int32), v((2, 1, 1), jnp.int32), v((25, H)), v((H,)),
-        v((128, 384)), v((384, 128)), v((384, 128)), v((8, 128)), v((16, 8, 128)),
+        v((128, 384)), v((384, 128)), v((384, 128)), v((8, 128)), v((16, 2, 1, 64), jnp.int32),
         v((384, 128)), v((25, EXT, 128)), v((EXT + 32, 128)), v((EXT, 128)), v((EXT, 128)),
         v((2048, 128), BF16),
         v((1024, 2048), BF16), v((8, 1024, 256), BF16), v((4, 2048, 256), BF16), v((H, 2048)),
         v((HALF, 128)), v((HALF, 128)), v((HALF, 128)), v((HALF, 128)),
         v((4, HALF, 256)), v((2, H, 256)),
-        v((PARTS, 16, PART, 128), BF16), v((2, PARTS, 16, PART, 128), BF16),
-        v((2, PARTS, 8, PART, 128), BF16), v((2, PARTS, 8, PART, 128), BF16),
-        v((2, PARTS, 8, PART, 128), BF16),
-        v((2, PARTS, 16, PART, 128), BF16), v((2, PARTS, 16, PART, 128), BF16),
+        v((PARTS, 16, MOST, 128), BF16), v((2, PARTS, 16, MOST, 128), BF16),
+        v((2, PARTS, 8, MOST, 128), BF16), v((2, PARTS, 8, MOST, 128), BF16),
+        v((2, PARTS, 8, MOST, 128), BF16),
+        v((2, PARTS, 16, MOST, 128), BF16), v((2, PARTS, 16, MOST, 128), BF16),
         v((HALF + 32, 128)), v((HALF, 128)),
-        v((3, PART, 128)), v((2, PART, 128)), v((PART, 128)),
+        v((3, HALO, 128)), v((2, HALO, 128)), v((HALO, 128)),
         v((HALF, 128)), v((HALF, 128)), v((HALF, 128)), v((HALF, 128)),
-        v((PARTS, 4, PART, 128), BF16),
-        sem((14,)), sem((15,)), sem((15,)), sem((8,)), sem((8,)), sem((1,)), sem((1,)), sem((4,)), sem((4,)),
+        v((PARTS, 4, MOST, 128), BF16),
+        sem((14,)), sem((12,)), sem((12,)), sem((PARTS,)), sem((PARTS,)), sem((PARTS,)), sem((PARTS,)), sem((8,)), sem((8,)), sem((1,)), sem((1,)), sem((4,)), sem((4,)),
         sem((3, PARTS)), sem((3, PARTS)), sem((2, PARTS)), sem((2, PARTS)), sem((2, PARTS)), sem((2, PARTS)),
         sem((2, PARTS)), sem((2, PARTS)),
     ]
-    dispatch, line_price, bus_price = pl.pallas_call(
+    both, line_price = pl.pallas_call(
         body,
         out_shape=(
-            jax.ShapeDtypeStruct((64, H), F32),
+            jax.ShapeDtypeStruct((2, 64, H), F32),
             jax.ShapeDtypeStruct((H, 512), F32),
-            jax.ShapeDtypeStruct((64, H), F32),
         ),
         in_specs=[hbm] * 14,
-        out_specs=(vmem,) * 3,
+        out_specs=(vmem,) * 2,
         scratch_shapes=scratch,
         compiler_params=pltpu.CompilerParams(
             collective_id=0, has_side_effects=True, vmem_limit_bytes=40 * 2**20),
@@ -444,7 +459,7 @@
         plant_counts[None],
         *map(in_hbm, (ramp_band, energy_price, load.T, ptdf, line_limit.T, line_price_start.T)),
     )
-    return dispatch, line_price.T, bus_price
+    return both[0], line_price.T, both[1]
 
 
 def solution(mesh):

time: 82 us -> 80.9 us (0.987)
    unnamed x3 -> x1, local copies, waits for them, and re-layouts: 2.1 us -> 0.81 us
where the time goes in v4:
time: 80.9 us; the launch traced here: 80.8 us
  Pallas kernels  78 us (96%)
  local copies, waits for them, and re-layouts  1.5 us (2%)
  between operations  1.29 us (2%)
    pallas_call x1, Pallas kernels, shards(): pl.pallas_call(body, out_shape=(jax.ShapeDtypeStruct((2, 64, H), F32), ja...  78 us

profile of v4, /device:TPU:1, one launch (start us, length us, event | category | flops | bytes accessed | tf_op | source)
XLA Modules:
  0.0 80.8 jit_solution(12345235202092154728)
XLA Ops:
  1.3 78.0 %dispatch_window.1 = (f32[2,64,288]{2,1,0:T(8,128)S(1)}, f32[288,512]{1,0:T(8,128)S(1)}) custom-call(f32[64,288]{1,0:T(8,128)} %dispatch_in.1, f32[64,288]{1,0:T(8,128)} %bus_price_in.1, f32[1,64]{1,0:T(1,128)} %bitcast.19, f32[1,64]{1,0:T(1,128)} %bitcast.20, f32[1,64]{1,0:T(1,128)} %bitcast.21, s32[1,64]{1,0:T(1,128)} %bitcast.22, s32[1,64]{1,0:T(1,128)} %bitcast.23, ...), custom_call_target="tpu_custom_call" | custom-call | tf_op jit(solution)/shard_map/dispatch_window/pallas_call | solution.py:444
  79.3 0.7 slice_bitcast_fusion
  80.0 0.8 %copy.19 = f32[512,288]{0,1:T(8,128)} copy(f32[512,288]{0,1:T(8,128)S(1)} %bitcast.15) | data formatting | bytes 1179648

commit v5 on v4

--- a/solution.py
+++ b/solution.py
@@ -68,6 +68,13 @@
 
     def offset(s, core):
         return pl.multiple_of(core * STARTS[s] + (1 - core) * (HALF - STARTS[s] - SIZES[s]), 16)
+
+    barrier = pltpu.get_barrier_semaphore()
+    peers = [sibling]
+    peers += [dev(z, chip(*d), core) for d in others for core in (c, other)]
+    peers += [dev((z + d) % 8, g, c) for d in range(1, 8)]
+    for peer in peers:
+        pl.semaphore_signal(barrier, inc=1, device_id=peer, device_id_type=pl.DeviceIdType.MESH)
 
     own_row = pl.multiple_of(HALF * c, 16)
     other_row = pl.multiple_of(HALF * other, 16)
@@ -96,34 +103,37 @@
     for copy in local:
         copy.start()
 
-    barrier = pltpu.get_barrier_semaphore()
-    peers = [sibling]
-    peers += [dev(z, chip(*d), core) for d in others for core in (c, other)]
-    peers += [dev((z + d) % 8, g, c) for d in range(1, 8)]
-    for peer in peers:
-        pl.semaphore_signal(barrier, inc=1, device_id=peer, device_id_type=pl.DeviceIdType.MESH)
-
     own_ext = pl.ds(pl.multiple_of(96 * c, 96), EXT)
+    stage[...] = jnp.zeros_like(stage)
+    vb[...] = jnp.zeros_like(vb)
+    vbe[...] = jnp.zeros_like(vbe)
     pl.semaphore_wait(barrier, len(peers))
     for i, (src, dst) in enumerate(cores):
         push(src, dst, cr_s.at[i], cr_r.at[i], sibling)
     for d in others:
         for core in (c, other):
             push(bus_in, ids.at[g, c], id_s.at[0], id_r.at[0], dev(z, chip(*d), core))
-    push(ptdf_in, pt.at[own_block], ex_s.at[3], ex_r.at[3], sibling)
-    push(limit_in.at[pl.ds(other_row, HALF), pl.ds(line_lane, 128)], slim, ex_s.at[4], ex_r.at[4], sibling)
-    push(lp_in.at[pl.ds(other_row, HALF), pl.ds(line_lane, 128)], slps, ex_s.at[5], ex_r.at[5], sibling)
+    push(ptdf_in, pt.at[own_block], ex_s.at[2], ex_r.at[2], sibling)
+    push(limit_in.at[pl.ds(other_row, HALF), pl.ds(line_lane, 128)], slim, ex_s.at[3], ex_r.at[3], sibling)
+    push(lp_in.at[pl.ds(other_row, HALF), pl.ds(line_lane, 128)], slps, ex_s.at[4], ex_r.at[4], sibling)
 
     def gather(grid, s, k):
         for d in others:
             block = grid.at[s, g, pl.ds(0, SIZES[s])]
-            push(block, block, ag_s.at[k, s], ag_r.at[k, s], dev(z, chip(*d), c))
+            push(block, block, ag_s.at[k], ag_r.at[k, s], dev(z, chip(*d), c))
 
     def gathered(grid, s, k):
         arrived(grid.at[s, pl.ds(0, 15), pl.ds(0, SIZES[s])], ag_r.at[k, s])
         return jnp.concatenate([grid[s, i, 0:SIZES[s]] for i in range(16)], axis=1)
 
-    for copy in local[:len(small)]:
+    local[0].wait()
+    arrived(cores_other[0], cr_r.at[0])
+    stage[:, 0:H] = pboth[...]
+    xp[...] = stage[...].T
+    for s in range(PARTS):
+        ga[s, g, 0:SIZES[s]] = xp[pl.ds(pl.multiple_of(own_row + offset(s, c), 16), SIZES[s])].astype(BF16)
+        gather(ga, s, 0)
+    for copy in local[1:len(small)]:
         copy.wait()
     for i in range(1, 7):
         arrived(cores_other[i], cr_r.at[i])
@@ -135,14 +145,6 @@
         ], axis=0) for i in (0, 1)], axis=1)
     for i in (0, 1):
         ids[g, i] = irow[i, 1:2]
-    arrived(cores_other[0], cr_r.at[0])
-    stage[...] = jnp.zeros_like(stage)
-    stage[:, 0:H] = pboth[...]
-    xp[...] = stage[...].T
-    for s in range(PARTS):
-        ga[s, g, 0:SIZES[s]] = xp[pl.ds(pl.multiple_of(own_row + offset(s, c), 16), SIZES[s])].astype(BF16)
-        gather(ga, s, 0)
-
     for copy in local[len(small):]:
         copy.wait()
     load_all = ld[...].astype(BF16)
@@ -151,7 +153,7 @@
         f0full[j] = lax.dot_general(load_all, block, NT, preferred_element_type=F32)
         f0[2 * c + j] = f0full[j, pl.ds(own_row, HALF)]
     own_pairs = pl.ds(2 * c, 2)
-    push(f0full.at[:, pl.ds(other_row, HALF)], f0.at[own_pairs], ex_s.at[11], ex_r.at[11], sibling)
+    push(f0full.at[:, pl.ds(other_row, HALF)], f0.at[own_pairs], ex_s.at[0], ex_r.at[0], sibling)
 
     stage[...] = jnp.zeros_like(stage)
     stage[0:25, 0:H] = ramp_v[...]
@@ -171,7 +173,7 @@
     bus_row = lax.broadcasted_iota(jnp.int32, (2048, 128), 0)
     oh[...] = jnp.where(bus_row == pm[4:5].astype(jnp.int32), 1.0, 0.0).astype(BF16)
 
-    arrived(pt.at[other_block], ex_r.at[3])
+    arrived(pt.at[other_block], ex_r.at[2])
     arrived(ids.at[pl.ds(0, 15)], id_r.at[0])
 
     def plant_columns(j, _):
@@ -180,7 +182,7 @@
         iota = lax.broadcasted_iota(jnp.int32, (2048, 256), 0)
         one_hot = jnp.where(iota == bus, 1.0, 0.0).astype(BF16)
         q[i] = jnp.dot(pt[...], one_hot, preferred_element_type=F32).astype(BF16)
-        push(q.at[i], q.at[i], q_s.at[j], q_r.at[j], sibling)
+        push(q.at[i], q.at[i], q_s.at[0], q_r.at[j], sibling)
         return 0
 
     core_row = pl.multiple_of(48 * c, 16)
@@ -192,12 +194,10 @@
     def price_part(s):
         px[ext_part(s)] = jnp.dot(gathered(ga, s, 0), oh[...], preferred_element_type=F32)
 
-    vb[...] = jnp.zeros_like(vb)
-    vbe[...] = jnp.zeros_like(vbe)
     lax.fori_loop(0, 2, plant_columns, 0)
     price_part(0)
     halo_s[0] = px[ext_part(0)]
-    push(halo_s.at[0], halo_p.at[0], ex_s.at[6], ex_r.at[6], sibling)
+    push(halo_s.at[0], halo_p.at[0], ex_s.at[5], ex_r.at[5], sibling)
     arrived(cores_other[7], cr_r.at[7])
     stage[:, 0:H] = dboth[...]
     xd[...] = stage[...].T
@@ -252,7 +252,7 @@
                 fb[k, s, 2 * pair + j, 0:n] = part[:, 128 * j:128 * j + 128].astype(BF16)
         for d in (4, 3, 5, 2, 6, 1, 7):
             target = (z + d) % 8
-            push(fb.at[k, s, target, pl.ds(0, n)], rc.at[k, s, z, pl.ds(0, n)], zr_s.at[k, s],
+            push(fb.at[k, s, target, pl.ds(0, n)], rc.at[k, s, z, pl.ds(0, n)], zr_s.at[k],
                  zr_r.at[k, s], dev(target, g, c))
 
     def limit_lines(k, s):
@@ -269,7 +269,7 @@
         sa[k, s, z, 0:n] = new.astype(BF16)
         block = sa.at[k, s, z, pl.ds(0, n)]
         for d in (4, 3, 5, 2, 6, 1, 7):
-            push(block, block, zg_s.at[k, s], zg_r.at[k, s], dev((z + d) % 8, g, c))
+            push(block, block, zg_s.at[k], zg_r.at[k, s], dev((z + d) % 8, g, c))
 
     def congestion(k, s):
         n = SIZES[s]
@@ -282,7 +282,7 @@
             pb[k, s, 2 * i + 1, 0:n] = part[:, 128:256]
         for dx, dy in others:
             to = chip(dx, dy)
-            push(pb.at[k, s, to, pl.ds(0, n)], rp.at[k, s, g, pl.ds(0, n)], rs_s.at[k, s], rs_r.at[k, s],
+            push(pb.at[k, s, to, pl.ds(0, n)], rp.at[k, s, g, pl.ds(0, n)], rs_s.at[k], rs_r.at[k, s],
                  dev(z, to, c))
 
     def prices(k, s):
@@ -297,21 +297,19 @@
     def drain(steps, refs):
         for ref, i in refs:
             sent_off(ref, ex_s.at[i])
-        for s in range(PARTS):
-            rows = pl.ds(0, SIZES[s])
-            for k in (0, 1) if 0 in steps else (2,):
-                sent_off(ga.at[s, pl.ds(0, 15), rows], ag_s.at[k, s])
-            for k in steps:
-                sent_off(rc.at[k, s, pl.ds(0, 7), rows], zr_s.at[k, s])
-                sent_off(sa.at[k, s, pl.ds(0, 7), rows], zg_s.at[k, s])
-                sent_off(rp.at[k, s, pl.ds(0, 15), rows], rs_s.at[k, s])
-            if 1 in steps:
-                sent_off(fin_s.at[rows], fin_ss.at[s])
-                sent_off(lr.at[s, :, rows], lr_s.at[s])
+        for k in (0, 1) if 0 in steps else (2,):
+            sent_off(ga.at[:, pl.ds(0, 15)], ag_s.at[k])
+        for k in steps:
+            sent_off(rc.at[k, :, pl.ds(0, 7)], zr_s.at[k])
+            sent_off(sa.at[k, :, pl.ds(0, 7)], zg_s.at[k])
+            sent_off(rp.at[k, :, pl.ds(0, 15)], rs_s.at[k])
+        if 1 in steps:
+            sent_off(fin_s, fin_ss.at[0])
+            sent_off(lr, lr_s.at[0])
 
     lax.fori_loop(2, 3 + no, plant_columns, 0)
     price_part(1)
-    arrived(halo_p.at[0], ex_r.at[6])
+    arrived(halo_p.at[0], ex_r.at[5])
     px[pl.ds(halo_at, HALO)] = halo_p[0]
     early_part(0)
     for s in range(2, PARTS):
@@ -319,14 +317,14 @@
     lax.fori_loop(0, ITERS, sweep, 0)
     other_parts(0)
     halo_s[1] = dsp[ext_part(0)]
-    push(halo_s.at[1], halo_d, ex_s.at[7], ex_r.at[7], sibling)
+    push(halo_s.at[1], halo_d, ex_s.at[5], ex_r.at[6], sibling)
     lax.fori_loop(3, 4 + no, plant_columns, 0)
-    arrived(slim, ex_r.at[4])
-    arrived(slps, ex_r.at[5])
+    arrived(slim, ex_r.at[3])
+    arrived(slps, ex_r.at[4])
     holds = c == z // 4
     lim[...] = jnp.where(holds, lim[...], slim[...])
     lps[...] = jnp.where(holds, lps[...], slps[...])
-    arrived(f0.at[pl.ds(2 * other, 2)], ex_r.at[11])
+    arrived(f0.at[pl.ds(2 * other, 2)], ex_r.at[0])
 
     def transpose_columns(j, core):
         i = 4 * core + j
@@ -346,11 +344,11 @@
         congestion(0, s)
     px[ext_part(0)] = prices(0, 0)
     halo_s[2] = px[ext_part(0)]
-    push(halo_s.at[2], halo_p.at[1], ex_s.at[8], ex_r.at[8], sibling)
-    arrived(halo_d, ex_r.at[7])
+    push(halo_s.at[2], halo_p.at[1], ex_s.at[5], ex_r.at[7], sibling)
+    arrived(halo_d, ex_r.at[6])
     dsp[pl.ds(halo_at, HALO)] = halo_d[...]
     px[ext_part(1)] = prices(0, 1)
-    arrived(halo_p.at[1], ex_r.at[8])
+    arrived(halo_p.at[1], ex_r.at[7])
     px[pl.ds(halo_at, HALO)] = halo_p[1]
 
     early_part(1)
@@ -359,7 +357,7 @@
     lax.fori_loop(0, ITERS, sweep, 0)
     other_parts(1)
     fd_s[...] = dsp[pl.ds(core_row, HALF)]
-    push(fd_s, fd_r, ex_s.at[9], ex_r.at[9], sibling)
+    push(fd_s, fd_r, ex_s.at[1], ex_r.at[1], sibling)
 
     def rows_out(mine, theirs):
         gap = jnp.zeros((96, 128), F32)
@@ -367,16 +365,14 @@
         second = jnp.where(c == 0, theirs, mine)
         return jnp.concatenate([first, second, gap], axis=0).T
 
-    arrived(fd_r, ex_r.at[9])
+    arrived(fd_r, ex_r.at[1])
     stage[...] = rows_out(fd_s[...], fd_r[...])
     both_out[0] = stage[own_lanes, 0:H]
     for i, (ref, _) in enumerate(cores):
         sent_off(ref, cr_s.at[i])
     sent_off(ids.at[pl.ds(0, 15)], id_s.at[0])
-    for j in range(4):
-        sent_off(q.at[j], q_s.at[j])
-    drain((0,), ((ptdf_in, 3), (slim, 4), (slps, 5), (f0.at[own_pairs], 11), (halo_s.at[0], 6), (halo_s.at[1], 7),
-                 (halo_s.at[2], 8)))
+    sent_off(q.at[pl.ds(0, 4)], q_s.at[0])
+    drain((0,), ((ptdf_in, 2), (slim, 3), (slps, 4), (f0.at[own_pairs], 0), (halo_s, 5)))
     for s in range(PARTS):
         flow(1, s)
     for s in range(PARTS):
@@ -384,7 +380,7 @@
     for s in range(PARTS):
         congestion(1, s)
     for s in range(PARTS):
-        push(sa.at[1, s, pl.ds(4 * other, 4), pl.ds(0, SIZES[s])], lr.at[s, :, pl.ds(0, SIZES[s])], lr_s.at[s],
+        push(sa.at[1, s, pl.ds(4 * other, 4), pl.ds(0, SIZES[s])], lr.at[s, :, pl.ds(0, SIZES[s])], lr_s.at[0],
              lr_r.at[s], sibling)
     for s in range(PARTS):
         rows = pl.ds(pl.multiple_of(own_row + offset(s, c), 16), SIZES[s])
@@ -393,7 +389,7 @@
     for s in range(PARTS):
         rows = pl.ds(offset(s, c), SIZES[s])
         fin_s[rows] = prices(1, s)
-        push(fin_s.at[rows], fin_r.at[rows], fin_ss.at[s], fin_rs.at[s], sibling)
+        push(fin_s.at[rows], fin_r.at[rows], fin_ss.at[0], fin_rs.at[s], sibling)
     for s in range(PARTS):
         arrived(lr.at[s, :, pl.ds(0, SIZES[s])], lr_r.at[s])
         rows = pl.ds(pl.multiple_of(other_row + offset(s, other), 16), SIZES[s])
@@ -404,7 +400,7 @@
     stage[...] = rows_out(fin_s[...], fin_r[...])
     both_out[1] = stage[own_lanes, 0:H]
 
-    drain((1,), ((fd_s, 9),))
+    drain((1,), ((fd_s, 1),))
 
 
 def shards(
@@ -437,9 +433,9 @@
         v((3, HALO, 128)), v((2, HALO, 128)), v((HALO, 128)),
         v((HALF, 128)), v((HALF, 128)), v((HALF, 128)), v((HALF, 128)),
         v((PARTS, 4, MOST, 128), BF16),
-        sem((14,)), sem((12,)), sem((12,)), sem((PARTS,)), sem((PARTS,)), sem((PARTS,)), sem((PARTS,)), sem((8,)), sem((8,)), sem((1,)), sem((1,)), sem((4,)), sem((4,)),
-        sem((3, PARTS)), sem((3, PARTS)), sem((2, PARTS)), sem((2, PARTS)), sem((2, PARTS)), sem((2, PARTS)),
-        sem((2, PARTS)), sem((2, PARTS)),
+        sem((14,)), sem((8,)), sem((8,)), sem((1,)), sem((PARTS,)), sem((1,)), sem((PARTS,)), sem((8,)), sem((8,)), sem((1,)), sem((1,)), sem((1,)), sem((4,)),
+        sem((3,)), sem((3, PARTS)), sem((2,)), sem((2, PARTS)), sem((2,)), sem((2, PARTS)),
+        sem((2,)), sem((2, PARTS)),
     ]
     both, line_price = pl.pallas_call(
         body,

time: 80.9 us -> 81.5 us (level)
  no operation moved by 1% of the time
where the time goes in v5:
time: 81.5 us; the launch traced here: 81.4 us
  Pallas kernels  78.6 us (96%)
  local copies, waits for them, and re-layouts  1.5 us (2%)
  between operations  1.29 us (2%)
    pallas_call x1, Pallas kernels, shards(): pl.pallas_call(body, out_shape=(jax.ShapeDtypeStruct((2, 64, H), F32), ja...  78.6 us

profile of v5, /device:TPU:1, one launch (start us, length us, event | category | flops | bytes accessed | tf_op | source)
XLA Modules:
  0.0 81.4 jit_solution(2251810197168221027)
XLA Ops:
  1.3 78.6 %dispatch_window.1 = (f32[2,64,288]{2,1,0:T(8,128)S(1)}, f32[288,512]{1,0:T(8,128)S(1)}) custom-call(f32[64,288]{1,0:T(8,128)} %dispatch_in.1, f32[64,288]{1,0:T(8,128)} %bus_price_in.1, f32[1,64]{1,0:T(1,128)} %bitcast.19, f32[1,64]{1,0:T(1,128)} %bitcast.20, f32[1,64]{1,0:T(1,128)} %bitcast.21, s32[1,64]{1,0:T(1,128)} %bitcast.22, s32[1,64]{1,0:T(1,128)} %bitcast.23, ...), custom_call_target="tpu_custom_call" | custom-call | tf_op jit(solution)/shard_map/dispatch_window/pallas_call | solution.py:440
  79.9 0.7 slice_bitcast_fusion
  80.6 0.8 %copy.19 = f32[512,288]{0,1:T(8,128)} copy(f32[512,288]{0,1:T(8,128)S(1)} %bitcast.15) | data formatting | bytes 1179648
